TPU v7x, 256 devices: a whole 4x4x8 slice. The times are simulated.
256 devices in a mesh: col: 32 (over y, x, core), row: 8 (over z).
Axes of the slice: x: 4, y: 4, z: 8, core: 2. Of those that a mesh axis runs over, the one named last changes fastest.
Arguments:
- rhs: bfloat16 [6, 32, 8, 128, 512], P(None, 'col', 'row'), may hold values from -6 to 6
- diag_inv: bfloat16 [6, 32, 8, 128, 128], P(None, 'col', 'row'), may hold values from -0.5 to 0.5
- factor: bfloat16 [5, 32, 8, 32, 2, 128, 128], P(None, 'col', 'row'), may hold values from -0.125 to 0.125
- columns: int32 [5, 32, 8, 32, 2], P(None, 'col', 'row'), may hold values from 0 to 7, as said below
Outputs:
- solution: bfloat16 [6, 32, 8, 128, 512], P(None, 'col', 'row')
Inputs may be any that keep to these rules, and one draw needn't show every extreme that they name: The 2 entries of columns for one factor row block and one column owner are distinct.
All inputs are finite; a program needn't handle non-finite values.
Results may differ from a plain program's by a relative error of at most 0.025.
Values may be sent and summed in bfloat16 or wider, within the bound.
No kernel may reach another device: no remote copies, remote signals or barrier semaphores. Data moves between devices by JAX's collectives and lax.ppermute only.
A program may use at most 128 MiB of HBM per device.

v0:
```python
import jax
import jax.numpy as jnp
from jax import lax
from jax.sharding import PartitionSpec as P


def from_everyone(shard, axis):
    size = lax.axis_size(axis)
    return lax.all_to_all(
        jnp.broadcast_to(shard[None], (size, *shard.shape)), axis, 0, 0, tiled=True
    )


def joined_along(parts, dim):
    dims = list(parts.shape[1:])
    dims[dim] *= parts.shape[0]
    return jnp.moveaxis(parts, 0, dim).reshape(dims)


def collect(shard, axis, dim):
    parts = from_everyone(shard, axis)
    return joined_along(parts, dim)


def in_blocks(shard, dim, size):
    dims = shard.shape
    parts = shard.reshape(*dims[:dim], size, dims[dim] // size, *dims[dim + 1 :])
    return jnp.moveaxis(parts, dim, 0)


def sent_and_summed(shard, axis, dim):
    size = lax.axis_size(axis)
    parts = lax.all_to_all(in_blocks(shard, dim, size), axis, 0, 0, tiled=True)
    return jnp.sum(parts.astype(jnp.float32), axis=0)


def solve_block(inverse, remainder):
    product = jnp.dot(
        inverse.astype(jnp.float32),
        remainder,
        precision=lax.Precision.HIGHEST,
        preferred_element_type=jnp.float32,
    )
    return product.astype(jnp.bfloat16)


def local_terms(blocks, selected, panels):
    chosen = jnp.take(panels, selected, axis=0)
    return jnp.einsum("tmab,tmbn->tan", blocks, chosen, preferred_element_type=jnp.float32)


def on_device(rhs, diag_inv, factor, columns):
    step_count = rhs.shape[0]
    panel_width = rhs.shape[-1]
    solved = []
    half_width = panel_width // 2
    remainders = [
        rhs[0, 0, 0, :, :half_width].astype(jnp.float32),
        rhs[0, 0, 0, :, half_width:].astype(jnp.float32),
    ]
    for step_index in range(step_count):
        current_pair = [
            solve_block(diag_inv[step_index, 0, 0], part_rest) for part_rest in remainders
        ]
        solved.append(jnp.concatenate(current_pair, axis=1))
        if step_index + 1 < step_count:
            following = []
            for member in range(2):
                panels = collect(current_pair[member][None], "row", 0)
                contrib = local_terms(factor[step_index, 0, 0], columns[step_index, 0, 0], panels)
                summed = sent_and_summed(contrib.astype(jnp.bfloat16), "col", 0)
                offset = member * half_width
                given = rhs[step_index + 1, 0, 0, :, offset : offset + half_width].astype(
                    jnp.float32
                )
                following.append(given - summed[0])
            remainders = following
    return jnp.stack(solved)[:, None, None]


def solution(mesh):
    return jax.shard_map(
        on_device,
        mesh=mesh,
        in_specs=(
            P(None, "col", "row", None, None),
            P(None, "col", "row", None, None),
            P(None, "col", "row", None, None, None, None),
            P(None, "col", "row", None, None),
        ),
        out_specs=P(None, "col", "row", None, None),
        check_vma=False,
    )
```

profile of v0, /device:TPU:1, one launch (start us, length us, event | category | flops | bytes accessed | tf_op | source)
XLA Modules:
  0.0 578.8 jit_solution(6202608117651558570)
XLA Ops:
  1.8 9.0 %all-to-all-start = ((bf16[8,1,128,256]{3,2,1,0:T(8,128)(2,1)}), bf16[8,1,128,256]{3,2,1,0:T(8,128)(2,1)S(1)}, u32[]{:S(2)}, u32[]{:S(2)}) async-start(bf16[8,1,128,256]{3,2,1,0:T(8,128)(2,1)} %broadcast_in_dim.31), calls=%async_computation | async-start | bytes 1048576 | tf_op jit(solution)/shard_map/all_to_all | solution.py:9
  11.9 16.9 %all-to-all-done = bf16[8,1,128,256]{3,2,1,0:T(8,128)(2,1)S(1)} async-done(((bf16[8,1,128,256]{3,2,1,0:T(8,128)(2,1)}), bf16[8,1,128,256]{3,2,1,0:T(8,128)(2,1)S(1)}, u32[]{:S(2)}, u32[]{:S(2)}) %all-to-all-start) | async-done | bytes 524320 | tf_op jit(solution)/shard_map/all_to_all | solution.py:9
  38.4 6.4 %copy.80 = bf16[32,2,128,256]{2,3,1,0:T(8,128)(2,1)} copy(bf16[32,2,128,256]{3,2,1,0:T(8,128)(2,1)} %bitcast.403) | data formatting | bytes 8388608 | tf_op jit(solution)/shard_map/jit(_take)/gather | solution.py:48
  51.0 7.6 %all-to-all-start.1 = ((bf16[32,1,128,256]{2,3,1,0:T(8,128)(2,1)}), bf16[32,1,128,256]{2,3,1,0:T(8,128)(2,1)S(1)}, u32[]{:S(2)}, u32[]{:S(2)}) async-start(bf16[32,1,128,256]{2,3,1,0:T(8,128)(2,1)} %fusion.30), calls=%async_computation.1 | async-start | bytes 4194304 | tf_op jit(solution)/shard_map/all_to_all | solution.py:33
  61.5 6.4 %copy.87 = bf16[32,2,128,256]{2,3,1,0:T(8,128)(2,1)} copy(bf16[32,2,128,256]{3,2,1,0:T(8,128)(2,1)} %bitcast.398) | data formatting | bytes 8388608 | tf_op jit(solution)/shard_map/jit(_take)/gather | solution.py:48
  73.4 13.0 %all-to-all-done.1 = bf16[32,1,128,256]{2,3,1,0:T(8,128)(2,1)S(1)} async-done(((bf16[32,1,128,256]{2,3,1,0:T(8,128)(2,1)}), bf16[32,1,128,256]{2,3,1,0:T(8,128)(2,1)S(1)}, u32[]{:S(2)}, u32[]{:S(2)}) %all-to-all-start.1) | async-done | bytes 2097184 | tf_op jit(solution)/shard_map/all_to_all | solution.py:33
  86.4 6.7 %all-to-all-start.3 = ((bf16[32,1,128,256]{2,3,1,0:T(8,128)(2,1)}), bf16[32,1,128,256]{2,3,1,0:T(8,128)(2,1)}, u32[]{:S(2)}, u32[]{:S(2)}) async-start(bf16[32,1,128,256]{2,3,1,0:T(8,128)(2,1)} %fusion.31), calls=%async_computation.3 | async-start | bytes 4194304 | tf_op jit(solution)/shard_map/all_to_all | solution.py:33
  95.8 25.4 %all-to-all-done.3 = bf16[32,1,128,256]{2,3,1,0:T(8,128)(2,1)} async-done(((bf16[32,1,128,256]{2,3,1,0:T(8,128)(2,1)}), bf16[32,1,128,256]{2,3,1,0:T(8,128)(2,1)}, u32[]{:S(2)}, u32[]{:S(2)}) %all-to-all-start.3) | async-done | bytes 2097184 | tf_op jit(solution)/shard_map/all_to_all | solution.py:33
  130.4 12.5 %all-to-all-done.4 = bf16[8,1,128,256]{3,2,1,0:T(8,128)(2,1)S(1)} async-done(((bf16[8,1,128,256]{3,2,1,0:T(8,128)(2,1)}), bf16[8,1,128,256]{3,2,1,0:T(8,128)(2,1)S(1)}, u32[]{:S(2)}, u32[]{:S(2)}) %all-to-all-start.4) | async-done | bytes 524320 | tf_op jit(solution)/shard_map/all_to_all | solution.py:9
  150.4 6.4 %copy.94 = bf16[32,2,128,256]{2,3,1,0:T(8,128)(2,1)} copy(bf16[32,2,128,256]{3,2,1,0:T(8,128)(2,1)} %bitcast.404) | data formatting | bytes 8388608 | tf_op jit(solution)/shard_map/jit(_take)/gather | solution.py:48
  162.4 11.5 %all-to-all-start.5 = ((bf16[32,1,128,256]{2,3,1,0:T(8,128)(2,1)}), bf16[32,1,128,256]{2,3,1,0:T(8,128)(2,1)S(1)}, u32[]{:S(2)}, u32[]{:S(2)}) async-start(bf16[32,1,128,256]{2,3,1,0:T(8,128)(2,1)} %fusion.32), calls=%async_computation.5 | async-start | bytes 4194304 | tf_op jit(solution)/shard_map/all_to_all | solution.py:33
  176.8 6.4 %copy.101 = bf16[32,2,128,256]{2,3,1,0:T(8,128)(2,1)} copy(bf16[32,2,128,256]{3,2,1,0:T(8,128)(2,1)} %bitcast.399) | data formatting | bytes 8388608 | tf_op jit(solution)/shard_map/jit(_take)/gather | solution.py:48
  188.7 13.0 %all-to-all-done.5 = bf16[32,1,128,256]{2,3,1,0:T(8,128)(2,1)S(1)} async-done(((bf16[32,1,128,256]{2,3,1,0:T(8,128)(2,1)}), bf16[32,1,128,256]{2,3,1,0:T(8,128)(2,1)S(1)}, u32[]{:S(2)}, u32[]{:S(2)}) %all-to-all-start.5) | async-done | bytes 2097184 | tf_op jit(solution)/shard_map/all_to_all | solution.py:33
  201.7 6.7 %all-to-all-start.7 = ((bf16[32,1,128,256]{2,3,1,0:T(8,128)(2,1)}), bf16[32,1,128,256]{2,3,1,0:T(8,128)(2,1)}, u32[]{:S(2)}, u32[]{:S(2)}) async-start(bf16[32,1,128,256]{2,3,1,0:T(8,128)(2,1)} %fusion.33), calls=%async_computation.7 | async-start | bytes 4194304 | tf_op jit(solution)/shard_map/all_to_all | solution.py:33
  209.2 27.2 %all-to-all-done.7 = bf16[32,1,128,256]{2,3,1,0:T(8,128)(2,1)} async-done(((bf16[32,1,128,256]{2,3,1,0:T(8,128)(2,1)}), bf16[32,1,128,256]{2,3,1,0:T(8,128)(2,1)}, u32[]{:S(2)}, u32[]{:S(2)}) %all-to-all-start.7) | async-done | bytes 2097184 | tf_op jit(solution)/shard_map/all_to_all | solution.py:33
  243.4 12.3 %all-to-all-done.8 = bf16[8,1,128,256]{3,2,1,0:T(8,128)(2,1)S(1)} async-done(((bf16[8,1,128,256]{3,2,1,0:T(8,128)(2,1)}), bf16[8,1,128,256]{3,2,1,0:T(8,128)(2,1)S(1)}, u32[]{:S(2)}, u32[]{:S(2)}) %all-to-all-start.8) | async-done | bytes 524320 | tf_op jit(solution)/shard_map/all_to_all | solution.py:9
  275.2 11.7 %all-to-all-start.9 = ((bf16[32,1,128,256]{2,3,1,0:T(8,128)(2,1)}), bf16[32,1,128,256]{2,3,1,0:T(8,128)(2,1)S(1)}, u32[]{:S(2)}, u32[]{:S(2)}) async-start(bf16[32,1,128,256]{2,3,1,0:T(8,128)(2,1)} %fusion.34), calls=%async_computation.9 | async-start | bytes 4194304 | tf_op jit(solution)/shard_map/all_to_all | solution.py:33
  301.7 13.0 %all-to-all-done.9 = bf16[32,1,128,256]{2,3,1,0:T(8,128)(2,1)S(1)} async-done(((bf16[32,1,128,256]{2,3,1,0:T(8,128)(2,1)}), bf16[32,1,128,256]{2,3,1,0:T(8,128)(2,1)S(1)}, u32[]{:S(2)}, u32[]{:S(2)}) %all-to-all-start.9) | async-done | bytes 2097184 | tf_op jit(solution)/shard_map/all_to_all | solution.py:33
  314.8 6.7 %all-to-all-start.11 = ((bf16[32,1,128,256]{2,3,1,0:T(8,128)(2,1)}), bf16[32,1,128,256]{2,3,1,0:T(8,128)(2,1)}, u32[]{:S(2)}, u32[]{:S(2)}) async-start(bf16[32,1,128,256]{2,3,1,0:T(8,128)(2,1)} %fusion.35), calls=%async_computation.11 | async-start | bytes 4194304 | tf_op jit(solution)/shard_map/all_to_all | solution.py:33
  322.2 27.3 %all-to-all-done.11 = bf16[32,1,128,256]{2,3,1,0:T(8,128)(2,1)} async-done(((bf16[32,1,128,256]{2,3,1,0:T(8,128)(2,1)}), bf16[32,1,128,256]{2,3,1,0:T(8,128)(2,1)}, u32[]{:S(2)}, u32[]{:S(2)}) %all-to-all-start.11) | async-done | bytes 2097184 | tf_op jit(solution)/shard_map/all_to_all | solution.py:33
  356.6 12.4 %all-to-all-done.12 = bf16[8,1,128,256]{3,2,1,0:T(8,128)(2,1)S(1)} async-done(((bf16[8,1,128,256]{3,2,1,0:T(8,128)(2,1)}), bf16[8,1,128,256]{3,2,1,0:T(8,128)(2,1)S(1)}, u32[]{:S(2)}, u32[]{:S(2)}) %all-to-all-start.12) | async-done | bytes 524320 | tf_op jit(solution)/shard_map/all_to_all | solution.py:9
  388.6 11.5 %all-to-all-start.13 = ((bf16[32,1,128,256]{2,3,1,0:T(8,128)(2,1)}), bf16[32,1,128,256]{2,3,1,0:T(8,128)(2,1)S(1)}, u32[]{:S(2)}, u32[]{:S(2)}) async-start(bf16[32,1,128,256]{2,3,1,0:T(8,128)(2,1)} %fusion.36), calls=%async_computation.13 | async-start | bytes 4194304 | tf_op jit(solution)/shard_map/all_to_all | solution.py:33
  402.9 6.4 %copy.129 = bf16[32,2,128,256]{2,3,1,0:T(8,128)(2,1)} copy(bf16[32,2,128,256]{3,2,1,0:T(8,128)(2,1)} %bitcast.401) | data formatting | bytes 8388608 | tf_op jit(solution)/shard_map/jit(_take)/gather | solution.py:48
  414.9 13.0 %all-to-all-done.13 = bf16[32,1,128,256]{2,3,1,0:T(8,128)(2,1)S(1)} async-done(((bf16[32,1,128,256]{2,3,1,0:T(8,128)(2,1)}), bf16[32,1,128,256]{2,3,1,0:T(8,128)(2,1)S(1)}, u32[]{:S(2)}, u32[]{:S(2)}) %all-to-all-start.13) | async-done | bytes 2097184 | tf_op jit(solution)/shard_map/all_to_all | solution.py:33
  427.9 6.9 %all-to-all-start.15 = ((bf16[32,1,128,256]{2,3,1,0:T(8,128)(2,1)}), bf16[32,1,128,256]{2,3,1,0:T(8,128)(2,1)}, u32[]{:S(2)}, u32[]{:S(2)}) async-start(bf16[32,1,128,256]{2,3,1,0:T(8,128)(2,1)} %fusion.37), calls=%async_computation.15 | async-start | bytes 4194304 | tf_op jit(solution)/shard_map/all_to_all | solution.py:33
  435.6 27.3 %all-to-all-done.15 = bf16[32,1,128,256]{2,3,1,0:T(8,128)(2,1)} async-done(((bf16[32,1,128,256]{2,3,1,0:T(8,128)(2,1)}), bf16[32,1,128,256]{2,3,1,0:T(8,128)(2,1)}, u32[]{:S(2)}, u32[]{:S(2)}) %all-to-all-start.15) | async-done | bytes 2097184 | tf_op jit(solution)/shard_map/all_to_all | solution.py:33
  470.0 12.4 %all-to-all-done.16 = bf16[8,1,128,256]{3,2,1,0:T(8,128)(2,1)S(1)} async-done(((bf16[8,1,128,256]{3,2,1,0:T(8,128)(2,1)}), bf16[8,1,128,256]{3,2,1,0:T(8,128)(2,1)S(1)}, u32[]{:S(2)}, u32[]{:S(2)}) %all-to-all-start.16) | async-done | bytes 524320 | tf_op jit(solution)/shard_map/all_to_all | solution.py:9
  501.9 11.5 %all-to-all-start.17 = ((bf16[32,1,128,256]{2,3,1,0:T(8,128)(2,1)}), bf16[32,1,128,256]{2,3,1,0:T(8,128)(2,1)S(1)}, u32[]{:S(2)}, u32[]{:S(2)}) async-start(bf16[32,1,128,256]{2,3,1,0:T(8,128)(2,1)} %fusion.38), calls=%async_computation.17 | async-start | bytes 4194304 | tf_op jit(solution)/shard_map/all_to_all | solution.py:33
  516.3 6.4 %copy.143 = bf16[32,2,128,256]{2,3,1,0:T(8,128)(2,1)} copy(bf16[32,2,128,256]{3,2,1,0:T(8,128)(2,1)} %bitcast.402) | data formatting | bytes 8388608 | tf_op jit(solution)/shard_map/jit(_take)/gather | solution.py:48
  528.3 13.0 %all-to-all-done.17 = bf16[32,1,128,256]{2,3,1,0:T(8,128)(2,1)S(1)} async-done(((bf16[32,1,128,256]{2,3,1,0:T(8,128)(2,1)}), bf16[32,1,128,256]{2,3,1,0:T(8,128)(2,1)S(1)}, u32[]{:S(2)}, u32[]{:S(2)}) %all-to-all-start.17) | async-done | bytes 2097184 | tf_op jit(solution)/shard_map/all_to_all | solution.py:33
  541.3 6.7 %all-to-all-start.19 = ((bf16[32,1,128,256]{2,3,1,0:T(8,128)(2,1)}), bf16[32,1,128,256]{2,3,1,0:T(8,128)(2,1)}, u32[]{:S(2)}, u32[]{:S(2)}) async-start(bf16[32,1,128,256]{2,3,1,0:T(8,128)(2,1)} %fusion.39), calls=%async_computation.19 | async-start | bytes 4194304 | tf_op jit(solution)/shard_map/all_to_all | solution.py:33
  552.1 23.8 %all-to-all-done.19 = bf16[32,1,128,256]{2,3,1,0:T(8,128)(2,1)} async-done(((bf16[32,1,128,256]{2,3,1,0:T(8,128)(2,1)}), bf16[32,1,128,256]{2,3,1,0:T(8,128)(2,1)}, u32[]{:S(2)}, u32[]{:S(2)}) %all-to-all-start.19) | async-done | bytes 2097184 | tf_op jit(solution)/shard_map/all_to_all | solution.py:33
  (165 shorter events, 180.4 us)
Async XLA Ops:
  1.8 27.0 %all-to-all-start = ((bf16[8,1,128,256]{3,2,1,0:T(8,128)(2,1)}), bf16[8,1,128,256]{3,2,1,0:T(8,128)(2,1)S(1)}, u32[]{:S(2)}, u32[]{:S(2)}) async-start(bf16[8,1,128,256]{3,2,1,0:T(8,128)(2,1)} %broadcast_in_dim.31), calls=%async_computation | async-start | bytes 1048576 | tf_op jit(solution)/shard_map/all_to_all | solution.py:9
  29.6 21.4 %all-to-all-start.2 = ((bf16[8,1,128,256]{3,2,1,0:T(8,128)(2,1)}), bf16[8,1,128,256]{3,2,1,0:T(8,128)(2,1)S(1)}, u32[]{:S(2)}, u32[]{:S(2)}) async-start(bf16[8,1,128,256]{3,2,1,0:T(8,128)(2,1)} %broadcast_in_dim.32), calls=%async_computation.2 | async-start | bytes 1048576 | tf_op jit(solution)/shard_map/all_to_all | solution.py:9
  51.0 35.4 %all-to-all-start.1 = ((bf16[32,1,128,256]{2,3,1,0:T(8,128)(2,1)}), bf16[32,1,128,256]{2,3,1,0:T(8,128)(2,1)S(1)}, u32[]{:S(2)}, u32[]{:S(2)}) async-start(bf16[32,1,128,256]{2,3,1,0:T(8,128)(2,1)} %fusion.30), calls=%async_computation.1 | async-start | bytes 4194304 | tf_op jit(solution)/shard_map/all_to_all | solution.py:33
  73.4 22.1 %copy-start = (bf16[6,1,1,128,128]{4,3,2,1,0:T(8,128)(2,1)S(1)}, bf16[6,1,1,128,128]{4,3,2,1,0:T(8,128)(2,1)}, u32[]{:S(2)}) copy-start(bf16[6,1,1,128,128]{4,3,2,1,0:T(8,128)(2,1)} %param.7) | copy-start | bytes 589828
  86.4 34.7 %all-to-all-start.3 = ((bf16[32,1,128,256]{2,3,1,0:T(8,128)(2,1)}), bf16[32,1,128,256]{2,3,1,0:T(8,128)(2,1)}, u32[]{:S(2)}, u32[]{:S(2)}) async-start(bf16[32,1,128,256]{2,3,1,0:T(8,128)(2,1)} %fusion.31), calls=%async_computation.3 | async-start | bytes 4194304 | tf_op jit(solution)/shard_map/all_to_all | solution.py:33
  122.0 20.9 %all-to-all-start.4 = ((bf16[8,1,128,256]{3,2,1,0:T(8,128)(2,1)}), bf16[8,1,128,256]{3,2,1,0:T(8,128)(2,1)S(1)}, u32[]{:S(2)}, u32[]{:S(2)}) async-start(bf16[8,1,128,256]{3,2,1,0:T(8,128)(2,1)} %broadcast_in_dim.33), calls=%async_computation.4 | async-start | bytes 1048576 | tf_op jit(solution)/shard_map/all_to_all | solution.py:9
  143.7 18.6 %all-to-all-start.6 = ((bf16[8,1,128,256]{3,2,1,0:T(8,128)(2,1)}), bf16[8,1,128,256]{3,2,1,0:T(8,128)(2,1)S(1)}, u32[]{:S(2)}, u32[]{:S(2)}) async-start(bf16[8,1,128,256]{3,2,1,0:T(8,128)(2,1)} %broadcast_in_dim.34), calls=%async_computation.6 | async-start | bytes 1048576 | tf_op jit(solution)/shard_map/all_to_all | solution.py:9
  162.4 39.4 %all-to-all-start.5 = ((bf16[32,1,128,256]{2,3,1,0:T(8,128)(2,1)}), bf16[32,1,128,256]{2,3,1,0:T(8,128)(2,1)S(1)}, u32[]{:S(2)}, u32[]{:S(2)}) async-start(bf16[32,1,128,256]{2,3,1,0:T(8,128)(2,1)} %fusion.32), calls=%async_computation.5 | async-start | bytes 4194304 | tf_op jit(solution)/shard_map/all_to_all | solution.py:33
  188.7 52.5 %copy-start.21 = (bf16[1,1,1,128,256]{4,3,2,1,0:T(8,128)(2,1)S(1)}, bf16[1,1,1,128,256]{4,3,2,1,0:T(8,128)(2,1)}, u32[]{:S(2)}) copy-start(bf16[1,1,1,128,256]{4,3,2,1,0:T(8,128)(2,1)} %get-tuple-element.11) | copy-start | bytes 196612
  201.7 34.6 %all-to-all-start.7 = ((bf16[32,1,128,256]{2,3,1,0:T(8,128)(2,1)}), bf16[32,1,128,256]{2,3,1,0:T(8,128)(2,1)}, u32[]{:S(2)}, u32[]{:S(2)}) async-start(bf16[32,1,128,256]{2,3,1,0:T(8,128)(2,1)} %fusion.33), calls=%async_computation.7 | async-start | bytes 4194304 | tf_op jit(solution)/shard_map/all_to_all | solution.py:33
  208.6 51.7 %copy-start.27 = (pred[32,2]{0,1:T(4,128)(4,1)S(1)}, pred[32,2]{0,1:T(4,128)(4,1)}, u32[]{:S(2)}) copy-start(pred[32,2]{0,1:T(4,128)(4,1)} %get-tuple-element.18) | copy-start | bytes 196
  209.1 28.0 %copy-start.3 = (bf16[128,256]{1,0:T(8,128)(2,1)}, bf16[128,256]{1,0:T(8,128)(2,1)S(1)}, u32[]{:S(2)}) copy-start(bf16[128,256]{1,0:T(8,128)(2,1)S(1)} %fusion.112) | copy-start | bytes 196612
  237.1 18.6 %all-to-all-start.8 = ((bf16[8,1,128,256]{3,2,1,0:T(8,128)(2,1)}), bf16[8,1,128,256]{3,2,1,0:T(8,128)(2,1)S(1)}, u32[]{:S(2)}, u32[]{:S(2)}) async-start(bf16[8,1,128,256]{3,2,1,0:T(8,128)(2,1)} %broadcast_in_dim.35), calls=%async_computation.8 | async-start | bytes 1048576 | tf_op jit(solution)/shard_map/all_to_all | solution.py:9
  256.6 18.6 %all-to-all-start.10 = ((bf16[8,1,128,256]{3,2,1,0:T(8,128)(2,1)}), bf16[8,1,128,256]{3,2,1,0:T(8,128)(2,1)S(1)}, u32[]{:S(2)}, u32[]{:S(2)}) async-start(bf16[8,1,128,256]{3,2,1,0:T(8,128)(2,1)} %broadcast_in_dim.36), calls=%async_computation.10 | async-start | bytes 1048576 | tf_op jit(solution)/shard_map/all_to_all | solution.py:9
  275.2 39.5 %all-to-all-start.9 = ((bf16[32,1,128,256]{2,3,1,0:T(8,128)(2,1)}), bf16[32,1,128,256]{2,3,1,0:T(8,128)(2,1)S(1)}, u32[]{:S(2)}, u32[]{:S(2)}) async-start(bf16[32,1,128,256]{2,3,1,0:T(8,128)(2,1)} %fusion.34), calls=%async_computation.9 | async-start | bytes 4194304 | tf_op jit(solution)/shard_map/all_to_all | solution.py:33
  301.7 52.6 %copy-start.19 = (bf16[1,1,1,128,256]{4,3,2,1,0:T(8,128)(2,1)S(1)}, bf16[1,1,1,128,256]{4,3,2,1,0:T(8,128)(2,1)}, u32[]{:S(2)}) copy-start(bf16[1,1,1,128,256]{4,3,2,1,0:T(8,128)(2,1)} %get-tuple-element.9) | copy-start | bytes 196612
  314.8 34.7 %all-to-all-start.11 = ((bf16[32,1,128,256]{2,3,1,0:T(8,128)(2,1)}), bf16[32,1,128,256]{2,3,1,0:T(8,128)(2,1)}, u32[]{:S(2)}, u32[]{:S(2)}) async-start(bf16[32,1,128,256]{2,3,1,0:T(8,128)(2,1)} %fusion.35), calls=%async_computation.11 | async-start | bytes 4194304 | tf_op jit(solution)/shard_map/all_to_all | solution.py:33
  321.6 52.0 %copy-start.26 = (pred[32,2]{0,1:T(4,128)(4,1)S(1)}, pred[32,2]{0,1:T(4,128)(4,1)}, u32[]{:S(2)}) copy-start(pred[32,2]{0,1:T(4,128)(4,1)} %get-tuple-element.17) | copy-start | bytes 196
  322.2 28.1 %copy-start.7 = (bf16[128,256]{1,0:T(8,128)(2,1)}, bf16[128,256]{1,0:T(8,128)(2,1)S(1)}, u32[]{:S(2)}) copy-start(bf16[128,256]{1,0:T(8,128)(2,1)S(1)} %fusion.114) | copy-start | bytes 196612
  350.3 18.8 %all-to-all-start.12 = ((bf16[8,1,128,256]{3,2,1,0:T(8,128)(2,1)}), bf16[8,1,128,256]{3,2,1,0:T(8,128)(2,1)S(1)}, u32[]{:S(2)}, u32[]{:S(2)}) async-start(bf16[8,1,128,256]{3,2,1,0:T(8,128)(2,1)} %broadcast_in_dim.68), calls=%async_computation.12 | async-start | bytes 1048576 | tf_op jit(solution)/shard_map/all_to_all | solution.py:9
  369.9 18.6 %all-to-all-start.14 = ((bf16[8,1,128,256]{3,2,1,0:T(8,128)(2,1)}), bf16[8,1,128,256]{3,2,1,0:T(8,128)(2,1)S(1)}, u32[]{:S(2)}, u32[]{:S(2)}) async-start(bf16[8,1,128,256]{3,2,1,0:T(8,128)(2,1)} %broadcast_in_dim.69), calls=%async_computation.14 | async-start | bytes 1048576 | tf_op jit(solution)/shard_map/all_to_all | solution.py:9
  388.6 39.4 %all-to-all-start.13 = ((bf16[32,1,128,256]{2,3,1,0:T(8,128)(2,1)}), bf16[32,1,128,256]{2,3,1,0:T(8,128)(2,1)S(1)}, u32[]{:S(2)}, u32[]{:S(2)}) async-start(bf16[32,1,128,256]{2,3,1,0:T(8,128)(2,1)} %fusion.36), calls=%async_computation.13 | async-start | bytes 4194304 | tf_op jit(solution)/shard_map/all_to_all | solution.py:33
  414.9 52.8 %copy-start.17 = (bf16[1,1,1,128,256]{4,3,2,1,0:T(8,128)(2,1)S(1)}, bf16[1,1,1,128,256]{4,3,2,1,0:T(8,128)(2,1)}, u32[]{:S(2)}) copy-start(bf16[1,1,1,128,256]{4,3,2,1,0:T(8,128)(2,1)} %get-tuple-element.7) | copy-start | bytes 196612
  427.9 34.9 %all-to-all-start.15 = ((bf16[32,1,128,256]{2,3,1,0:T(8,128)(2,1)}), bf16[32,1,128,256]{2,3,1,0:T(8,128)(2,1)}, u32[]{:S(2)}, u32[]{:S(2)}) async-start(bf16[32,1,128,256]{2,3,1,0:T(8,128)(2,1)} %fusion.37), calls=%async_computation.15 | async-start | bytes 4194304 | tf_op jit(solution)/shard_map/all_to_all | solution.py:33
  435.0 52.0 %copy-start.25 = (pred[32,2]{0,1:T(4,128)(4,1)S(1)}, pred[32,2]{0,1:T(4,128)(4,1)}, u32[]{:S(2)}) copy-start(pred[32,2]{0,1:T(4,128)(4,1)} %get-tuple-element.16) | copy-start | bytes 196
  435.5 28.1 %copy-start.11 = (bf16[128,256]{1,0:T(8,128)(2,1)}, bf16[128,256]{1,0:T(8,128)(2,1)S(1)}, u32[]{:S(2)}) copy-start(bf16[128,256]{1,0:T(8,128)(2,1)S(1)} %fusion.116) | copy-start | bytes 196612
  463.7 18.8 %all-to-all-start.16 = ((bf16[8,1,128,256]{3,2,1,0:T(8,128)(2,1)}), bf16[8,1,128,256]{3,2,1,0:T(8,128)(2,1)S(1)}, u32[]{:S(2)}, u32[]{:S(2)}) async-start(bf16[8,1,128,256]{3,2,1,0:T(8,128)(2,1)} %broadcast_in_dim.70), calls=%async_computation.16 | async-start | bytes 1048576 | tf_op jit(solution)/shard_map/all_to_all | solution.py:9
  483.3 18.6 %all-to-all-start.18 = ((bf16[8,1,128,256]{3,2,1,0:T(8,128)(2,1)}), bf16[8,1,128,256]{3,2,1,0:T(8,128)(2,1)S(1)}, u32[]{:S(2)}, u32[]{:S(2)}) async-start(bf16[8,1,128,256]{3,2,1,0:T(8,128)(2,1)} %broadcast_in_dim.71), calls=%async_computation.18 | async-start | bytes 1048576 | tf_op jit(solution)/shard_map/all_to_all | solution.py:9
  501.9 39.4 %all-to-all-start.17 = ((bf16[32,1,128,256]{2,3,1,0:T(8,128)(2,1)}), bf16[32,1,128,256]{2,3,1,0:T(8,128)(2,1)S(1)}, u32[]{:S(2)}, u32[]{:S(2)}) async-start(bf16[32,1,128,256]{2,3,1,0:T(8,128)(2,1)} %fusion.38), calls=%async_computation.17 | async-start | bytes 4194304 | tf_op jit(solution)/shard_map/all_to_all | solution.py:33
  528.3 22.6 %copy-start.12 = (bf16[128,256]{1,0:T(8,128)(2,1)S(1)}, bf16[128,256]{1,0:T(8,128)(2,1)}, u32[]{:S(2)}) copy-start(bf16[128,256]{1,0:T(8,128)(2,1)} %copy-done.11) | copy-start | bytes 196612
  528.3 22.6 %copy-start.14 = (bf16[128,256]{1,0:T(8,128)(2,1)S(1)}, bf16[128,256]{1,0:T(8,128)(2,1)}, u32[]{:S(2)}) copy-start(bf16[128,256]{1,0:T(8,128)(2,1)} %copy-done.13) | copy-start | bytes 196612
  541.3 34.7 %all-to-all-start.19 = ((bf16[32,1,128,256]{2,3,1,0:T(8,128)(2,1)}), bf16[32,1,128,256]{2,3,1,0:T(8,128)(2,1)}, u32[]{:S(2)}, u32[]{:S(2)}) async-start(bf16[32,1,128,256]{2,3,1,0:T(8,128)(2,1)} %fusion.39), calls=%async_computation.19 | async-start | bytes 4194304 | tf_op jit(solution)/shard_map/all_to_all | solution.py:33
  (16 other events, 275.2 us)
where the time goes:
time: 582 us; the launch traced here: 579 us
  waiting for transfers between devices  263 us (45%)
  starting transfers between devices  132 us (23%)
  local copies, waits for them, and re-layouts  106 us (18%)
  matrix products  59.8 us (10%)
  other arithmetic  17 us (3%)
    all_to_all x10, waiting for transfers between devices, sent_and_summed(): parts = lax.all_to_all(in_blocks(shard, dim, size), axis, 0, 0, tiled=True)  196 us
    gather x20, local copies, waits for them, and re-layouts, local_terms(): chosen = jnp.take(panels, selected, axis=0)  92.7 us
    all_to_all x10, starting transfers between devices, sent_and_summed(): parts = lax.all_to_all(in_blocks(shard, dim, size), axis, 0, 0, tiled=True)  87.7 us
    all_to_all x10, waiting for transfers between devices, from_everyone(): lax.all_to_all(jnp.broadcast_to(shard[None], (size, *shard.shape)), axis,...  67.3 us
    dot_general x10, matrix products, local_terms(): jnp.einsum('tmab,tmbn->tan', blocks, chosen, preferred_element_type=jnp.f...  55.5 us
    all_to_all x10, starting transfers between devices, from_everyone(): lax.all_to_all(jnp.broadcast_to(shard[None], (size, *shard.shape)), axis,...  44.8 us
  transfers between devices with their start and end apart: 20, of which 16 were waited for; matrix products, arithmetic and copies ran while one was open for 29% of the time, Pallas kernels for 0%

commit v1 on v0

v1 whole, which is shorter than its diff:
```python
import functools

import jax
import jax.numpy as jnp
from jax import lax
from jax.experimental import pallas as pl
from jax.experimental.pallas import tpu as pltpu
from jax.sharding import Mesh
from jax.sharding import PartitionSpec as P

CORES = 2
TARGET_BLOCK = 8
SOURCE_BLOCK = 4
VMEM_LIMIT = 40 * 1024 * 1024


def times_inverse(inverse, remainder):
    high = remainder.astype(jnp.bfloat16)
    rest = remainder - high.astype(jnp.float32)
    middle = rest.astype(jnp.bfloat16)
    low = (rest - middle.astype(jnp.float32)).astype(jnp.bfloat16)
    dot = functools.partial(jnp.dot, inverse, preferred_element_type=jnp.float32)
    return (dot(low) + dot(middle) + dot(high)).astype(jnp.bfloat16)


def store_solved(mine, other, inv_mine, inv_other, copies_ref, solved_ref):
    for slot, (remainder, inverse) in enumerate(((mine, inv_mine), (other, inv_other))):
        panel = times_inverse(inverse, remainder)
        solved_ref[slot] = panel
        for peer in range(copies_ref.shape[0]):
            copies_ref[peer, slot] = panel


def first_kernel(core_ref, rhs_ref, rhs_other_ref, inv_ref, inv_other_ref, copies_ref, solved_ref):
    store_solved(
        rhs_ref[0, 0, 0].astype(jnp.float32),
        rhs_other_ref[0].astype(jnp.float32),
        inv_ref[0, 0, 0],
        inv_other_ref[0, 0, 0],
        copies_ref,
        solved_ref,
    )


def next_kernel(
    core_ref, terms_ref, rhs_ref, rhs_other_ref, inv_ref, inv_other_ref, copies_ref, solved_ref, total
):
    step = pl.program_id(0)
    part = jnp.sum(terms_ref[...].astype(jnp.float32), axis=0)

    @pl.when(step == 0)
    def _():
        total[...] = part

    @pl.when(step > 0)
    def _():
        total[...] += part

    @pl.when(step == pl.num_programs(0) - 1)
    def _():
        store_solved(
            rhs_ref[0, 0, 0].astype(jnp.float32) - total[0],
            rhs_other_ref[0].astype(jnp.float32) - total[1],
            inv_ref[0, 0, 0],
            inv_other_ref[0, 0, 0],
            copies_ref,
            solved_ref,
        )


def solve(level, core, terms, rhs, rhs_other, inv, inv_other, peers):
    _, _, _, blk, width = rhs.shape
    half = width // CORES
    steps = 1 if terms is None else terms.shape[0] // SOURCE_BLOCK
    level_specs = [
        pl.BlockSpec((1, 1, 1, blk, half), lambda i, c: (level, 0, 0, 0, c[0])),
        pl.BlockSpec((1, blk, half), lambda i, c: (level, 0, 0)),
        pl.BlockSpec((1, 1, 1, blk, blk), lambda i, c: (level, 0, 0, 0, 0)),
        pl.BlockSpec((1, 1, 1, blk, blk), lambda i, c: (level, 0, 0, 0, 0)),
    ]
    term_specs = [pl.BlockSpec((SOURCE_BLOCK, CORES, blk, half), lambda i, c: (i, 0, 0, 0))]
    operands = (rhs, rhs_other, inv, inv_other)
    return pl.pallas_call(
        first_kernel if terms is None else next_kernel,
        out_shape=(
            jax.ShapeDtypeStruct((peers, CORES, blk, half), jnp.bfloat16),
            jax.ShapeDtypeStruct((CORES, blk, half), jnp.bfloat16),
        ),
        grid_spec=pltpu.PrefetchScalarGridSpec(
            num_scalar_prefetch=1,
            grid=(steps,),
            in_specs=level_specs if terms is None else term_specs + level_specs,
            out_specs=(
                pl.BlockSpec((peers, CORES, blk, half), lambda i, c: (0, 0, 0, 0)),
                pl.BlockSpec((CORES, blk, half), lambda i, c: (0, 0, 0)),
            ),
            scratch_shapes=[] if terms is None else [pltpu.VMEM((CORES, blk, half), jnp.float32)],
        ),
        compiler_params=pltpu.CompilerParams(vmem_limit_bytes=VMEM_LIMIT),
        name="solve_panels",
    )(core, *(operands if terms is None else (terms, *operands)))


def terms_kernel(level, slots, core_ref, cols_ref, cols_other_ref, panels_ref, mine_ref, other_ref, out_ref):
    core = core_ref[0]
    step = pl.program_id(0)
    block = mine_ref.shape[3]
    targets = block * pl.num_programs(0)
    for chip in range(block // CORES):
        for slot in range(CORES):
            local = CORES * chip + (core if slot == 0 else 1 - core)
            place = (level * targets + step * block + local) * slots
            left, right = [], []
            for which, (blocks, cols) in enumerate(((mine_ref, cols_ref), (other_ref, cols_other_ref))):
                for m in range(slots):
                    left.append(blocks[0, 0, 0, local, m])
                    right.append(panels_ref[cols[place + m], which])
            product = jnp.dot(
                jnp.concatenate(left, axis=1),
                jnp.concatenate(right, axis=0),
                preferred_element_type=jnp.float32,
            )
            out_ref[chip, slot] = product.astype(jnp.bfloat16)


def terms(level, core, cols, cols_other, panels, factor, factor_other):
    _, _, _, targets, slots, blk, _ = factor.shape
    half = panels.shape[-1]
    factor_spec = pl.BlockSpec(
        (1, 1, 1, TARGET_BLOCK, slots, blk, blk), lambda i, *_: (level, 0, 0, i, 0, 0, 0)
    )
    return pl.pallas_call(
        functools.partial(terms_kernel, level, slots),
        out_shape=jax.ShapeDtypeStruct((targets // CORES, CORES, blk, half), jnp.bfloat16),
        grid_spec=pltpu.PrefetchScalarGridSpec(
            num_scalar_prefetch=3,
            grid=(targets // TARGET_BLOCK,),
            in_specs=[
                pl.BlockSpec(panels.shape, lambda i, *_: (0, 0, 0, 0)),
                factor_spec,
                factor_spec,
            ],
            out_specs=pl.BlockSpec(
                (TARGET_BLOCK // CORES, CORES, blk, half), lambda i, *_: (i, 0, 0, 0)
            ),
        ),
        compiler_params=pltpu.CompilerParams(vmem_limit_bytes=VMEM_LIMIT),
        name="level_terms",
    )(core, cols, cols_other, panels, factor, factor_other)


def on_device(rhs, diag_inv, factor, columns):
    levels = rhs.shape[0]
    half = rhs.shape[-1] // CORES
    peers = lax.axis_size("row")
    here = lax.axis_index("core").astype(jnp.int32)
    core = here.reshape(1)
    swap = functools.partial(lax.ppermute, axis_name="core", perm=[(0, 1), (1, 0)])

    theirs = lax.dynamic_slice_in_dim(rhs[:, 0, 0], (1 - here) * half, half, axis=2)
    rhs_other = swap(theirs)
    inv_other = swap(diag_inv)
    cols = columns.reshape(-1)
    cols_other = swap(cols)
    factor_other = swap(factor)

    solved = []
    received = None
    for level in range(levels):
        copies, panel = solve(level, core, received, rhs, rhs_other, diag_inv, inv_other, peers)
        solved.append(panel)
        if level + 1 < levels:
            panels = lax.all_to_all(copies, "row", 0, 0, tiled=True)
            partial = terms(level, core, cols, cols_other, panels, factor, factor_other)
            received = lax.all_to_all(partial, "chip", 0, 0, tiled=True)

    def whole(panels):
        mine = jnp.stack([p[0] for p in panels])
        other = swap(jnp.stack([p[1] for p in panels]))
        return jnp.where(
            here == 0,
            jnp.concatenate([mine, other], axis=-1),
            jnp.concatenate([other, mine], axis=-1),
        )

    out = jnp.concatenate([whole(solved[:-1]), whole(solved[-1:])], axis=0)
    return out[:, None, None]


def solution(mesh):
    cols, rows = mesh.devices.shape
    fine = Mesh(mesh.devices.reshape(cols // CORES, CORES, rows), ("chip", "core", "row"))
    owner = ("chip", "core")
    return jax.shard_map(
        on_device,
        mesh=fine,
        in_specs=(
            P(None, owner, "row", None, None),
            P(None, owner, "row", None, None),
            P(None, owner, "row", None, None, None, None),
            P(None, owner, "row", None, None),
        ),
        out_specs=P(None, owner, "row", None, None),
        check_vma=False,
    )
```

time: 582 us -> 372 us (0.64)
  blocking collectives: 0 us -> 234 us
  waiting for transfers between devices: 263 us -> 53.6 us
  starting transfers between devices: 132 us -> 28.8 us
  local copies, waits for them, and re-layouts: 106 us -> 22.8 us
  matrix products: 59.8 us -> 0 us
  Pallas kernels: 0 us -> 29 us
  other arithmetic: 17 us -> 2.44 us
    all_to_all x0 -> x8, blocking collectives: none -> 234 us  [the longest x4 118 us: on_device(): received = lax.all_to_all(partial, 'chip', 0, 0, tiled=True)]
    all_to_all x20 -> x2, waiting for transfers between devices: 263 us -> 37.9 us  [the longest x1 27.7 us: on_device(): panels = lax.all_to_all(copies, 'row', 0, 0, tiled=True)]
    all_to_all x20 -> x2, starting transfers between devices: 132 us -> 10.4 us  [the longest x1 6.45 us: on_device(): panels = lax.all_to_all(copies, 'row', 0, 0, tiled=True)]
    gather x20 -> x0, local copies, waits for them, and re-layouts: 92.7 us -> none  [local_terms(): chosen = jnp.take(panels, selected, axis=0)]
    dot_general x22 -> x0, matrix products: 59.8 us -> none  [the longest x10 55.5 us: local_terms(): jnp.einsum('tmab,tmbn->tan', blocks, chosen, preferred_element_type=jnp.f...]
    pallas_call x0 -> x11, Pallas kernels: none -> 29 us  [the longest x5 22.4 us: terms(): pl.pallas_call(functools.partial(terms_kernel, level, slots), out_shape=j...]
    unnamed x66 -> x45, local copies, waits for them, and re-layouts: 1.22 us -> 20.1 us
    ppermute x0 -> x6, starting transfers between devices: none -> 18.4 us  [the longest x2 14.1 us: whole(): other = swap(jnp.stack([p[1] for p in panels]))]
  transfers between devices with their start and end apart: 20 -> 8, of which waited for: 16 -> 5; matrix products, arithmetic and copies ran while one was open for 29% -> 3% of each run, Pallas kernels for 0% -> 1%
where the time goes in v1:
time: 372 us; the launch traced here: 371 us
  blocking collectives  234 us (63%)
  waiting for transfers between devices  53.6 us (14%)
  Pallas kernels  29 us (8%)
  starting transfers between devices  28.8 us (8%)
  local copies, waits for them, and re-layouts  22.8 us (6%)
    all_to_all x4, blocking collectives, on_device(): received = lax.all_to_all(partial, 'chip', 0, 0, tiled=True)  118 us
    all_to_all x4, blocking collectives, on_device(): panels = lax.all_to_all(copies, 'row', 0, 0, tiled=True)  117 us
    all_to_all x1, waiting for transfers between devices, on_device(): panels = lax.all_to_all(copies, 'row', 0, 0, tiled=True)  27.7 us
    pallas_call x5, Pallas kernels, terms(): pl.pallas_call(functools.partial(terms_kernel, level, slots), out_shape=j...  22.4 us
    unnamed x45, local copies, waits for them, and re-layouts  20.1 us
    ppermute x1, waiting for transfers between devices, on_device(): inv_other = swap(diag_inv)  14.8 us
    ppermute x2, starting transfers between devices, whole(): other = swap(jnp.stack([p[1] for p in panels]))  14.1 us
    all_to_all x1, waiting for transfers between devices, on_device(): received = lax.all_to_all(partial, 'chip', 0, 0, tiled=True)  10.2 us
  transfers between devices with their start and end apart: 8, of which 5 were waited for; matrix products, arithmetic and copies ran while one was open for 3% of the time, Pallas kernels for 1%

profile of v1, /device:TPU:1, one launch (start us, length us, event | category | flops | bytes accessed | tf_op | source)
XLA Modules:
  0.0 371.2 jit_solution(1658941404842100540)
XLA Ops:
  0.0 3.2 collective-permute-start.3
  4.9 14.8 %collective-permute-done.1.inv_other_ref = bf16[6,1,1,128,128]{4,3,2,1,0:T(8,128)(2,1)S(1)} collective-permute-done((bf16[6,1,1,128,128]{4,3,2,1,0:T(8,128)(2,1)}, bf16[6,1,1,128,128]{4,3,2,1,0:T(8,128)(2,1)S(1)}, u32[]{:S(2)}, u32[]{:S(2)}) %collective-permute-start.1) | collective-permute-done | bytes 196640 | tf_op jit(solution)/shard_map/ppermute | solution.py:162
  19.7 1.3 copy-done.2
  22.0 1.3 solve_panels.6
  23.9 6.5 %all-to-all-start = ((bf16[8,2,128,256]{3,2,1,0:T(8,128)(2,1)}), bf16[8,2,128,256]{3,2,1,0:T(8,128)(2,1)S(1)}, u32[]{:S(2)}, u32[]{:S(2)}) async-start(bf16[8,2,128,256]{3,2,1,0:T(8,128)(2,1)} %get-tuple-element.17), calls=%async_computation | async-start | bytes 2097152 | tf_op jit(solution)/shard_map/all_to_all | solution.py:173
  32.0 27.7 %all-to-all-done.panels_ref = bf16[8,2,128,256]{3,2,1,0:T(8,128)(2,1)S(1)} async-done(((bf16[8,2,128,256]{3,2,1,0:T(8,128)(2,1)}), bf16[8,2,128,256]{3,2,1,0:T(8,128)(2,1)S(1)}, u32[]{:S(2)}, u32[]{:S(2)}) %all-to-all-start) | async-done | bytes 1048608 | tf_op jit(solution)/shard_map/all_to_all | solution.py:173
  60.6 4.0 %copy-done = bf16[5,1,1,32,2,128,128]{6,5,4,3,2,1,0:T(8,128)(2,1)S(1)} copy-done((bf16[5,1,1,32,2,128,128]{6,5,4,3,2,1,0:T(8,128)(2,1)S(1)}, bf16[5,1,1,32,2,128,128]{6,5,4,3,2,1,0:T(8,128)(2,1)}, u32[]{:S(2)}) %copy-start) | copy-done | bytes 10485784
  65.8 4.8 %level_terms.5 = bf16[16,2,128,256]{3,2,1,0:T(8,128)(2,1)S(1)} custom-call(s32[1]{0:T(128)} %bitcast.core_ref, s32[320]{0:T(512)S(1)} %reshape.60.cols_ref, s32[320]{0:T(512)S(1)} %collective-permute-done.2.cols_other_ref, bf16[8,2,128,256]{3,2,1,0:T(8,128)(2,1)S(1)} %copy-done.13, bf16[5,1,1,32,2,128,128]{6,5,4,3,2,1,0:T(8,128)(2,1)S(1)} %copy-done, ...), custom_call_target="tpu_custom_call" | custom-call | tf_op jit(solution)/shard_map/level_terms/pallas_call | solution.py:132
  70.7 1.4 copy-done.7
  72.0 34.3 %all_to_all.50.terms_ref = bf16[16,2,128,256]{3,2,1,0:T(8,128)(2,1)S(1)} all-to-all(bf16[16,2,128,256]{3,2,1,0:T(8,128)(2,1)} %copy-done.7), channel_id=1, replica_groups=mesh['chip'=16,'core'=2,'row'=8] {'chip'}, dimensions={0} | all-to-all | bytes 4194304 | tf_op jit(solution)/shard_map/all_to_all | solution.py:175
  107.9 28.3 %all_to_all.51.panels_ref = bf16[8,2,128,256]{3,2,1,0:T(8,128)(2,1)S(1)} all-to-all(bf16[8,2,128,256]{3,2,1,0:T(8,128)(2,1)S(1)} %get-tuple-element.19), channel_id=1, replica_groups=mesh['chip'=16,'core'=2,'row'=8] {'row'}, dimensions={0} | all-to-all | bytes 2097152 | tf_op jit(solution)/shard_map/all_to_all | solution.py:173
  136.2 4.1 %level_terms.6 = bf16[16,2,128,256]{3,2,1,0:T(8,128)(2,1)S(1)} custom-call(s32[1]{0:T(128)} %bitcast.core_ref, s32[320]{0:T(512)S(1)} %reshape.60.cols_ref, s32[320]{0:T(512)S(1)} %collective-permute-done.2.cols_other_ref, bf16[8,2,128,256]{3,2,1,0:T(8,128)(2,1)S(1)} %all_to_all.51.panels_ref, bf16[5,1,1,32,2,128,128]{6,5,4,3,2,1,0:T(8,128)(2,1)S(1)} %copy-done.1, ...), custom_call_target="tpu_custom_call" | custom-call | tf_op jit(solution)/shard_map/level_terms/pallas_call | solution.py:132
  140.4 29.4 %all_to_all.52.terms_ref = bf16[16,2,128,256]{3,2,1,0:T(8,128)(2,1)S(1)} all-to-all(bf16[16,2,128,256]{3,2,1,0:T(8,128)(2,1)S(1)} %level_terms.6), channel_id=1, replica_groups=mesh['chip'=16,'core'=2,'row'=8] {'chip'}, dimensions={0} | all-to-all | bytes 4194304 | tf_op jit(solution)/shard_map/all_to_all | solution.py:175
  171.3 29.8 %all_to_all.53.panels_ref = bf16[8,2,128,256]{3,2,1,0:T(8,128)(2,1)S(1)} all-to-all(bf16[8,2,128,256]{3,2,1,0:T(8,128)(2,1)S(1)} %get-tuple-element.21), channel_id=1, replica_groups=mesh['chip'=16,'core'=2,'row'=8] {'row'}, dimensions={0} | all-to-all | bytes 2097152 | tf_op jit(solution)/shard_map/all_to_all | solution.py:173
  201.1 4.1 %level_terms.7 = bf16[16,2,128,256]{3,2,1,0:T(8,128)(2,1)S(1)} custom-call(s32[1]{0:T(128)} %bitcast.core_ref, s32[320]{0:T(512)S(1)} %reshape.60.cols_ref, s32[320]{0:T(512)S(1)} %collective-permute-done.2.cols_other_ref, bf16[8,2,128,256]{3,2,1,0:T(8,128)(2,1)S(1)} %all_to_all.53.panels_ref, bf16[5,1,1,32,2,128,128]{6,5,4,3,2,1,0:T(8,128)(2,1)S(1)} %copy-done.1, ...), custom_call_target="tpu_custom_call" | custom-call | tf_op jit(solution)/shard_map/level_terms/pallas_call | solution.py:132
  205.2 27.9 %all_to_all.54.terms_ref = bf16[16,2,128,256]{3,2,1,0:T(8,128)(2,1)S(1)} all-to-all(bf16[16,2,128,256]{3,2,1,0:T(8,128)(2,1)S(1)} %level_terms.7), channel_id=1, replica_groups=mesh['chip'=16,'core'=2,'row'=8] {'chip'}, dimensions={0} | all-to-all | bytes 4194304 | tf_op jit(solution)/shard_map/all_to_all | solution.py:175
  234.6 29.6 %all_to_all.55.panels_ref = bf16[8,2,128,256]{3,2,1,0:T(8,128)(2,1)S(1)} all-to-all(bf16[8,2,128,256]{3,2,1,0:T(8,128)(2,1)S(1)} %get-tuple-element.23), channel_id=1, replica_groups=mesh['chip'=16,'core'=2,'row'=8] {'row'}, dimensions={0} | all-to-all | bytes 2097152 | tf_op jit(solution)/shard_map/all_to_all | solution.py:173
  264.2 4.1 %level_terms.8 = bf16[16,2,128,256]{3,2,1,0:T(8,128)(2,1)S(1)} custom-call(s32[1]{0:T(128)} %bitcast.core_ref, s32[320]{0:T(512)S(1)} %reshape.60.cols_ref, s32[320]{0:T(512)S(1)} %collective-permute-done.2.cols_other_ref, bf16[8,2,128,256]{3,2,1,0:T(8,128)(2,1)S(1)} %all_to_all.55.panels_ref, bf16[5,1,1,32,2,128,128]{6,5,4,3,2,1,0:T(8,128)(2,1)S(1)} %copy-done.1, ...), custom_call_target="tpu_custom_call" | custom-call | tf_op jit(solution)/shard_map/level_terms/pallas_call | solution.py:132
  268.3 25.9 %all_to_all.56.terms_ref = bf16[16,2,128,256]{3,2,1,0:T(8,128)(2,1)S(1)} all-to-all(bf16[16,2,128,256]{3,2,1,0:T(8,128)(2,1)S(1)} %level_terms.8), channel_id=1, replica_groups=mesh['chip'=16,'core'=2,'row'=8] {'chip'}, dimensions={0} | all-to-all | bytes 4194304 | tf_op jit(solution)/shard_map/all_to_all | solution.py:175
  295.7 29.1 %all_to_all.57.panels_ref = bf16[8,2,128,256]{3,2,1,0:T(8,128)(2,1)S(1)} all-to-all(bf16[8,2,128,256]{3,2,1,0:T(8,128)(2,1)S(1)} %get-tuple-element.25), channel_id=1, replica_groups=mesh['chip'=16,'core'=2,'row'=8] {'row'}, dimensions={0} | all-to-all | bytes 2097152 | tf_op jit(solution)/shard_map/all_to_all | solution.py:173
  324.8 5.2 %level_terms.9 = bf16[16,2,128,256]{3,2,1,0:T(8,128)(2,1)} custom-call(s32[1]{0:T(128)} %bitcast.core_ref, s32[320]{0:T(512)S(1)} %reshape.60.cols_ref, s32[320]{0:T(512)S(1)} %collective-permute-done.2.cols_other_ref, bf16[8,2,128,256]{3,2,1,0:T(8,128)(2,1)S(1)} %all_to_all.57.panels_ref, bf16[5,1,1,32,2,128,128]{6,5,4,3,2,1,0:T(8,128)(2,1)S(1)} %copy-done.1, ...), custom_call_target="tpu_custom_call" | custom-call | tf_op jit(solution)/shard_map/level_terms/pallas_call | solution.py:132
  330.0 3.9 %all-to-all-start.9 = ((bf16[16,2,128,256]{3,2,1,0:T(8,128)(2,1)}), bf16[16,2,128,256]{3,2,1,0:T(8,128)(2,1)S(1)}, u32[]{:S(2)}, u32[]{:S(2)}) async-start(bf16[16,2,128,256]{3,2,1,0:T(8,128)(2,1)} %level_terms.9), calls=%async_computation.9 | async-start | bytes 4194304 | tf_op jit(solution)/shard_map/all_to_all | solution.py:175
  334.0 1.5 slice_dynamic-update-slice_fusion.9
  335.5 1.5 slice_dynamic-update-slice_fusion.8
  337.0 1.5 slice_dynamic-update-slice_fusion.7
  338.5 1.5 slice_dynamic-update-slice_fusion.6
  340.1 1.5 slice_dynamic-update-slice_fusion.5
  341.6 6.1 %collective-permute-start.4 = (bf16[5,128,256]{2,1,0:T(8,128)(2,1)}, bf16[5,128,256]{2,1,0:T(8,128)(2,1)}, u32[]{:S(2)}, u32[]{:S(2)}) collective-permute-start(bf16[5,128,256]{2,1,0:T(8,128)(2,1)} %get-tuple-element.28), channel_id=1, source_target_pairs={{0,8},{8,0},{1,9},{9,1},{2,10},{10,2},{3,11},{11,3},{4,12},{12,4},... | collective-permute-start | bytes 983048 | tf_op jit(solution)/shard_map/ppermute | solution.py:179
  347.7 10.2 %all-to-all-done.9.terms_ref = bf16[16,2,128,256]{3,2,1,0:T(8,128)(2,1)S(1)} async-done(((bf16[16,2,128,256]{3,2,1,0:T(8,128)(2,1)}), bf16[16,2,128,256]{3,2,1,0:T(8,128)(2,1)S(1)}, u32[]{:S(2)}, u32[]{:S(2)}) %all-to-all-start.9) | async-done | bytes 2097184 | tf_op jit(solution)/shard_map/all_to_all | solution.py:175
  358.9 1.8 solve_panels.11
  360.8 8.0 %collective-permute-start.5 = (bf16[1,128,256]{2,1,0:T(8,128)(2,1)S(1)}, bf16[1,128,256]{2,1,0:T(8,128)(2,1)S(1)}, u32[]{:S(2)}, u32[]{:S(2)}) collective-permute-start(bf16[1,128,256]{2,1,0:T(8,128)(2,1)S(1)} %get-tuple-element.38), channel_id=1, source_target_pairs={{0,8},{8,0},{1,9},{9,1},{2,10},{10,2},{3,11},{11,3},{4,12},{12,4},... | collective-permute-start | bytes 196616 | tf_op jit(solution)/shard_map/ppermute | solution.py:179
  368.7 1.5 maximum_select_fusion
  (55 shorter events, 15.0 us)
Async XLA Ops:
  0.0 60.6 %collective-permute-start.3 = (bf16[5,1,1,32,2,128,128]{6,5,4,3,2,1,0:T(8,128)(2,1)}, bf16[5,1,1,32,2,128,128]{6,5,4,3,2,1,0:T(8,128)(2,1)}, u32[]{:S(2)}, u32[]{:S(2)}) collective-permute-start(bf16[5,1,1,32,2,128,128]{6,5,4,3,2,1,0:T(8,128)(2,1)} %mine_ref.9), channel_id=1, source_target_pairs={{0,8},{8,0},{1,9},{9,1},{2,10},{10,2},{3,11},{11,3},{4,12},{12,4},... | collective-permute-start | bytes 31457288 | tf_op jit(solution)/shard_map/ppermute | solution.py:165
  3.2 27.1 %copy-start.19 = (s32[5,1,1,32,2]{3,4,2,1,0:T(2,128)S(1)}, s32[5,1,1,32,2]{3,4,2,1,0:T(2,128)}, u32[]{:S(2)}) copy-start(s32[5,1,1,32,2]{3,4,2,1,0:T(2,128)} %param.7) | copy-start | bytes 3844
  4.3 15.5 %collective-permute-start = (bf16[6,128,256]{2,1,0:T(8,128)(2,1)S(1)}, bf16[6,128,256]{2,1,0:T(8,128)(2,1)S(1)}, u32[]{:S(2)}, u32[]{:S(2)}) collective-permute-start(bf16[6,128,256]{2,1,0:T(8,128)(2,1)S(1)} %dynamic-slice_bitcast_fusion), channel_id=1, source_target_pairs={{0,8},{8,0},{1,9},{9,1},{2,10},{10,2},{3,11},{11,3},{4,12},{12,4},... | collective-permute-start | bytes 1179656 | tf_op jit(solution)/shard_map/ppermute | solution.py:161
  4.4 15.3 %collective-permute-start.1 = (bf16[6,1,1,128,128]{4,3,2,1,0:T(8,128)(2,1)}, bf16[6,1,1,128,128]{4,3,2,1,0:T(8,128)(2,1)S(1)}, u32[]{:S(2)}, u32[]{:S(2)}) collective-permute-start(bf16[6,1,1,128,128]{4,3,2,1,0:T(8,128)(2,1)} %inv_ref.11), channel_id=1, source_target_pairs={{0,8},{8,0},{1,9},{9,1},{2,10},{10,2},{3,11},{11,3},{4,12},{12,4},... | collective-permute-start | bytes 589832 | tf_op jit(solution)/shard_map/ppermute | solution.py:162
  19.7 274.6 %copy-start.10 = (bf16[6,1,1,128,128]{4,3,2,1,0:T(8,128)(2,1)}, bf16[6,1,1,128,128]{4,3,2,1,0:T(8,128)(2,1)S(1)}, u32[]{:S(2)}) copy-start(bf16[6,1,1,128,128]{4,3,2,1,0:T(8,128)(2,1)S(1)} %collective-permute-done.1.inv_other_ref) | copy-start | bytes 589828
  19.7 3.5 copy-start.4
  19.7 1.3 copy-start.2
  21.0 0.9 copy-start.8
  23.3 0.6 copy-start.14
  23.9 35.7 %all-to-all-start = ((bf16[8,2,128,256]{3,2,1,0:T(8,128)(2,1)}), bf16[8,2,128,256]{3,2,1,0:T(8,128)(2,1)S(1)}, u32[]{:S(2)}, u32[]{:S(2)}) async-start(bf16[8,2,128,256]{3,2,1,0:T(8,128)(2,1)} %get-tuple-element.17), calls=%async_computation | async-start | bytes 2097152 | tf_op jit(solution)/shard_map/all_to_all | solution.py:173
  30.6 1.3 collective-permute-start.2
  59.7 1.0 copy-start.12
  60.6 4.0 %copy-start = (bf16[5,1,1,32,2,128,128]{6,5,4,3,2,1,0:T(8,128)(2,1)S(1)}, bf16[5,1,1,32,2,128,128]{6,5,4,3,2,1,0:T(8,128)(2,1)}, u32[]{:S(2)}) copy-start(bf16[5,1,1,32,2,128,128]{6,5,4,3,2,1,0:T(8,128)(2,1)} %mine_ref.9) | copy-start | bytes 31457284
  64.6 1.2 copy-start.13
  65.8 70.4 %copy-start.1 = (bf16[5,1,1,32,2,128,128]{6,5,4,3,2,1,0:T(8,128)(2,1)S(1)}, bf16[5,1,1,32,2,128,128]{6,5,4,3,2,1,0:T(8,128)(2,1)}, u32[]{:S(2)}) copy-start(bf16[5,1,1,32,2,128,128]{6,5,4,3,2,1,0:T(8,128)(2,1)} %mine_ref.9) | copy-start | bytes 31457284
  70.7 1.4 copy-start.7
  72.0 34.3 %copy-start.3 = (bf16[6,1,1,128,512]{4,3,2,1,0:T(8,128)(2,1)S(1)}, bf16[6,1,1,128,512]{4,3,2,1,0:T(8,128)(2,1)}, u32[]{:S(2)}) copy-start(bf16[6,1,1,128,512]{4,3,2,1,0:T(8,128)(2,1)} %rhs_ref.11) | copy-start | bytes 2359300
  72.0 34.3 %copy-start.5 = (bf16[6,128,256]{2,1,0:T(8,128)(2,1)S(1)}, bf16[6,128,256]{2,1,0:T(8,128)(2,1)}, u32[]{:S(2)}) copy-start(bf16[6,128,256]{2,1,0:T(8,128)(2,1)} %copy-done.4) | copy-start | bytes 1179652
  72.0 34.3 %copy-start.9 = (bf16[6,1,1,128,128]{4,3,2,1,0:T(8,128)(2,1)S(1)}, bf16[6,1,1,128,128]{4,3,2,1,0:T(8,128)(2,1)}, u32[]{:S(2)}) copy-start(bf16[6,1,1,128,128]{4,3,2,1,0:T(8,128)(2,1)} %inv_ref.11) | copy-start | bytes 589828
  107.3 0.6 copy-start.15
  170.6 0.6 copy-start.16
  234.0 0.6 copy-start.17
  295.1 0.6 copy-start.18
  330.0 27.9 %copy-start.6 = (bf16[6,128,256]{2,1,0:T(8,128)(2,1)S(1)}, bf16[6,128,256]{2,1,0:T(8,128)(2,1)}, u32[]{:S(2)}) copy-start(bf16[6,128,256]{2,1,0:T(8,128)(2,1)} %copy-done.4) | copy-start | bytes 1179652
  330.0 27.9 %all-to-all-start.9 = ((bf16[16,2,128,256]{3,2,1,0:T(8,128)(2,1)}), bf16[16,2,128,256]{3,2,1,0:T(8,128)(2,1)S(1)}, u32[]{:S(2)}, u32[]{:S(2)}) async-start(bf16[16,2,128,256]{3,2,1,0:T(8,128)(2,1)} %level_terms.9), calls=%async_computation.9 | async-start | bytes 4194304 | tf_op jit(solution)/shard_map/all_to_all | solution.py:175
  341.6 27.1 %collective-permute-start.4 = (bf16[5,128,256]{2,1,0:T(8,128)(2,1)}, bf16[5,128,256]{2,1,0:T(8,128)(2,1)}, u32[]{:S(2)}, u32[]{:S(2)}) collective-permute-start(bf16[5,128,256]{2,1,0:T(8,128)(2,1)} %get-tuple-element.28), channel_id=1, source_target_pairs={{0,8},{8,0},{1,9},{9,1},{2,10},{10,2},{3,11},{11,3},{4,12},{12,4},... | collective-permute-start | bytes 983048 | tf_op jit(solution)/shard_map/ppermute | solution.py:179
  358.0 0.9 copy-start.11
  360.8 9.4 %collective-permute-start.5 = (bf16[1,128,256]{2,1,0:T(8,128)(2,1)S(1)}, bf16[1,128,256]{2,1,0:T(8,128)(2,1)S(1)}, u32[]{:S(2)}, u32[]{:S(2)}) collective-permute-start(bf16[1,128,256]{2,1,0:T(8,128)(2,1)S(1)} %get-tuple-element.38), channel_id=1, source_target_pairs={{0,8},{8,0},{1,9},{9,1},{2,10},{10,2},{3,11},{11,3},{4,12},{12,4},... | collective-permute-start | bytes 196616 | tf_op jit(solution)/shard_map/ppermute | solution.py:179

commit v2 on v0

v2 whole, which is shorter than its diff:
```python
import functools

import jax
import jax.numpy as jnp
from jax import lax
from jax.experimental import pallas as pl
from jax.experimental.pallas import tpu as pltpu
from jax.sharding import Mesh
from jax.sharding import PartitionSpec as P

CORES = 2
CHIP_BLOCK = 4
STAGGER = 36
VMEM_LIMIT = 16 * 1024 * 1024
VMEM = pl.BlockSpec(memory_space=pltpu.VMEM)
SMEM = pl.BlockSpec(memory_space=pltpu.SMEM)
PARAMS = pltpu.CompilerParams(vmem_limit_bytes=VMEM_LIMIT)


def times_inverse(inverse, remainder):
    high = remainder.astype(jnp.bfloat16)
    rest = remainder - high.astype(jnp.float32)
    middle = rest.astype(jnp.bfloat16)
    low = (rest - middle.astype(jnp.float32)).astype(jnp.bfloat16)
    dot = functools.partial(jnp.dot, inverse, preferred_element_type=jnp.float32)
    return (dot(low) + dot(middle) + dot(high)).astype(jnp.bfloat16)


def store_solved(slot, inverse, remainder, copies_ref, solved_ref):
    panel = times_inverse(inverse, remainder)
    solved_ref[slot] = panel
    for peer in range(copies_ref.shape[0]):
        copies_ref[peer, slot] = panel


def first_kernel(core_ref, rhs_ref, inv_ref, copies_ref, solved_ref):
    def once(_, carry):
        for slot in range(CORES):
            store_solved(
                slot, inv_ref[slot], rhs_ref[slot].astype(jnp.float32), copies_ref, solved_ref
            )
        return carry

    lax.fori_loop(0, 1 + (1 - core_ref[0]) * STAGGER, once, 0)


def next_kernel(terms_ref, rhs_ref, inv_ref, *out_refs):
    for slot in range(CORES):
        total = terms_ref[0, slot].astype(jnp.float32)
        for chip in range(1, terms_ref.shape[0]):
            total += terms_ref[chip, slot].astype(jnp.float32)
        remainder = rhs_ref[slot].astype(jnp.float32) - total
        if len(out_refs) == 2:
            store_solved(slot, inv_ref[slot], remainder, *out_refs)
        else:
            out_refs[0][slot] = times_inverse(inv_ref[slot], remainder)


def solve(core, terms, rhs, inv, peers):
    solved = jax.ShapeDtypeStruct(rhs.shape, jnp.bfloat16)
    copies = jax.ShapeDtypeStruct((peers, *rhs.shape), jnp.bfloat16)
    if terms is None:
        return pl.pallas_call(
            first_kernel,
            out_shape=(copies, solved),
            in_specs=[SMEM, VMEM, VMEM],
            out_specs=(VMEM, VMEM),
            compiler_params=PARAMS,
            name="first_panels",
        )(core, rhs, inv)
    return pl.pallas_call(
        next_kernel,
        out_shape=(copies, solved) if peers else solved,
        in_specs=[VMEM, VMEM, VMEM],
        out_specs=(VMEM, VMEM) if peers else VMEM,
        compiler_params=PARAMS,
        name="solve_panels",
    )(terms, rhs, inv)


def terms_kernel(level, core_ref, cols_ref, cols_other_ref, panels_ref, mine_ref, other_ref, out_ref):
    core = core_ref[0]
    targets, slots = mine_ref.shape[:2]

    def some_chips(block, carry):
        for chip in range(CHIP_BLOCK):
            for slot in range(CORES):
                target = CORES * (block * CHIP_BLOCK + chip) + (core if slot == 0 else 1 - core)
                place = (level * targets + target) * slots
                left, right = [], []
                for which, (blocks, cols) in enumerate(
                    ((mine_ref, cols_ref), (other_ref, cols_other_ref))
                ):
                    for m in range(slots):
                        left.append(blocks[target, m])
                        right.append(panels_ref[cols[place + m], which])
                product = jnp.dot(
                    jnp.concatenate(left, axis=1),
                    jnp.concatenate(right, axis=0),
                    preferred_element_type=jnp.float32,
                )
                out_ref[block * CHIP_BLOCK + chip, slot] = product.astype(jnp.bfloat16)
        return carry

    lax.fori_loop(0, targets // CORES // CHIP_BLOCK, some_chips, 0)


def terms(level, core, cols, cols_other, panels, mine, other):
    targets = mine.shape[0]
    return pl.pallas_call(
        functools.partial(terms_kernel, level),
        out_shape=jax.ShapeDtypeStruct((targets // CORES, *panels.shape[1:]), jnp.bfloat16),
        in_specs=[SMEM, SMEM, SMEM, VMEM, VMEM, VMEM],
        out_specs=VMEM,
        compiler_params=PARAMS,
        name="level_terms",
    )(core, cols, cols_other, panels, mine, other)


def on_device(rhs, diag_inv, factor, columns):
    levels = rhs.shape[0]
    half = rhs.shape[-1] // CORES
    peers = lax.axis_size("row")
    here = lax.axis_index("core").astype(jnp.int32)
    core = here.reshape(1)
    swap = functools.partial(lax.ppermute, axis_name="core", perm=[(0, 1), (1, 0)])

    rhs_here = lax.dynamic_slice_in_dim(rhs[:, 0, 0], here * half, half, axis=2)
    rhs_other = swap(lax.dynamic_slice_in_dim(rhs[:, 0, 0], (1 - here) * half, half, axis=2))
    inv_other = swap(diag_inv)
    columns_other = swap(columns)
    large, rhs_other, inv_other, columns_other = lax.optimization_barrier(
        (factor, rhs_other, inv_other, columns_other)
    )
    factor_other = swap(large)
    rhs_pair = jnp.stack([rhs_here, rhs_other], axis=1)
    inv_pair = jnp.stack([diag_inv[:, 0, 0], inv_other[:, 0, 0]], axis=1)
    cols, cols_other = columns.reshape(-1), columns_other.reshape(-1)

    solved = []
    received = None
    for level in range(levels):
        last = level + 1 == levels
        result = solve(core, received, rhs_pair[level], inv_pair[level], 0 if last else peers)
        if last:
            solved.append(result)
            break
        copies, panel = result
        solved.append(panel)
        panels = lax.all_to_all(copies, "row", 0, 0, tiled=True)
        partial = terms(
            level, core, cols, cols_other, panels, factor[level, 0, 0], factor_other[level, 0, 0]
        )
        received = lax.all_to_all(partial, "chip", 0, 0, tiled=True)

    def whole(panels):
        mine = jnp.stack([p[0] for p in panels])
        other = swap(jnp.stack([p[1] for p in panels]))
        return jnp.where(
            here == 0,
            jnp.concatenate([mine, other], axis=-1),
            jnp.concatenate([other, mine], axis=-1),
        )

    out = jnp.concatenate([whole(solved[:-1]), whole(solved[-1:])], axis=0)
    return out[:, None, None]


def solution(mesh):
    cols, rows = mesh.devices.shape
    fine = Mesh(mesh.devices.reshape(cols // CORES, CORES, rows), ("chip", "core", "row"))
    owner = ("chip", "core")
    return jax.shard_map(
        on_device,
        mesh=fine,
        in_specs=(
            P(None, owner, "row", None, None),
            P(None, owner, "row", None, None),
            P(None, owner, "row", None, None, None, None),
            P(None, owner, "row", None, None),
        ),
        out_specs=P(None, owner, "row", None, None),
        check_vma=False,
    )
```

time: 582 us -> 276 us (0.47)
  waiting for transfers between devices: 263 us -> 2.81 us
  blocking collectives: 0 us -> 170 us
  local copies, waits for them, and re-layouts: 106 us -> 26.6 us
  starting transfers between devices: 132 us -> 56.1 us
  matrix products: 59.8 us -> 0 us
  Pallas kernels: 0 us -> 16.6 us
  other arithmetic: 17 us -> 3.48 us
    all_to_all x20 -> x2, waiting for transfers between devices: 263 us -> 0.74 us  [the longest x1 0.73 us: on_device(): panels = lax.all_to_all(copies, 'row', 0, 0, tiled=True)]
    all_to_all x0 -> x8, blocking collectives: none -> 170 us  [the longest x4 85.2 us: on_device(): received = lax.all_to_all(partial, 'chip', 0, 0, tiled=True)]
    all_to_all x20 -> x2, starting transfers between devices: 132 us -> 10.3 us  [the longest x1 6.45 us: on_device(): panels = lax.all_to_all(copies, 'row', 0, 0, tiled=True)]
    gather x20 -> x0, local copies, waits for them, and re-layouts: 92.7 us -> none  [local_terms(): chosen = jnp.take(panels, selected, axis=0)]
    dot_general x22 -> x0, matrix products: 59.8 us -> none  [the longest x10 55.5 us: local_terms(): jnp.einsum('tmab,tmbn->tan', blocks, chosen, preferred_element_type=jnp.f...]
    ppermute x0 -> x6, starting transfers between devices: none -> 45.8 us  [the longest x2 41.6 us: whole(): other = swap(jnp.stack([p[1] for p in panels]))]
    pallas_call x0 -> x11, Pallas kernels: none -> 16.6 us  [the longest x5 12.1 us: terms(): pl.pallas_call(functools.partial(terms_kernel, level), out_shape=jax.Shap...]
    squeeze x0 -> x2, local copies, waits for them, and re-layouts: none -> 15.1 us  [the longest x1 7.56 us: on_device(): factor_other[level, 0, 0]]
  transfers between devices with their start and end apart: 20 -> 8, of which waited for: 16 -> 3; matrix products, arithmetic and copies ran while one was open for 29% -> 8% of each run, Pallas kernels for 0% -> 1%
where the time goes in v2:
time: 276 us
  blocking collectives  170 us (62%)
  starting transfers between devices  56.1 us (20%)
  local copies, waits for them, and re-layouts  26.6 us (10%)
  Pallas kernels  16.6 us (6%)
  other arithmetic  3.48 us (1%)
  waiting for transfers between devices  2.81 us (1%)
    all_to_all x4, blocking collectives, on_device(): received = lax.all_to_all(partial, 'chip', 0, 0, tiled=True)  85.2 us
    all_to_all x4, blocking collectives, on_device(): panels = lax.all_to_all(copies, 'row', 0, 0, tiled=True)  84.7 us
    ppermute x2, starting transfers between devices, whole(): other = swap(jnp.stack([p[1] for p in panels]))  41.6 us
    pallas_call x5, Pallas kernels, terms(): pl.pallas_call(functools.partial(terms_kernel, level), out_shape=jax.Shap...  12.1 us
    unnamed x45, local copies, waits for them, and re-layouts  7.89 us
    squeeze x1, local copies, waits for them, and re-layouts, on_device(): factor_other[level, 0, 0]  7.56 us
    squeeze x1, local copies, waits for them, and re-layouts, on_device(): factor[level, 0, 0]  7.49 us
    all_to_all x1, starting transfers between devices, on_device(): panels = lax.all_to_all(copies, 'row', 0, 0, tiled=True)  6.45 us
  transfers between devices with their start and end apart: 8, of which 3 were waited for; matrix products, arithmetic and copies ran while one was open for 8% of the time, Pallas kernels for 1%

profile of v2, /device:TPU:1, one launch (start us, length us, event | category | flops | bytes accessed | tf_op | source)
XLA Modules:
  0.0 275.7 jit_solution(7162002577171514332)
XLA Ops:
  0.0 1.2 dynamic-slice_bitcast_fusion.1
  1.2 3.3 %collective-permute-start = (bf16[6,128,256]{2,1,0:T(8,128)(2,1)S(1)}, bf16[6,128,256]{2,1,0:T(8,128)(2,1)S(1)}, u32[]{:S(2)}, u32[]{:S(2)}) collective-permute-start(bf16[6,128,256]{2,1,0:T(8,128)(2,1)S(1)} %get-tuple-element.50), channel_id=1, source_target_pairs={{0,8},{8,0},{1,9},{9,1},{2,10},{10,2},{3,11},{11,3},{4,12},{12,4},... | collective-permute-start | bytes 1179656 | tf_op jit(solution)/shard_map/ppermute | solution.py:129
  5.0 1.3 collective-permute-done.2
  6.7 1.6 fusion.21
  8.3 0.8 fusion.10
  9.1 1.3 first_panels.1
  11.0 6.4 %all-to-all-start = ((bf16[8,2,128,256]{3,2,1,0:T(8,128)(2,1)}), bf16[8,2,128,256]{3,2,1,0:T(8,128)(2,1)S(1)}, u32[]{:S(2)}, u32[]{:S(2)}) async-start(bf16[8,2,128,256]{3,2,1,0:T(8,128)(2,1)} %get-tuple-element.23), calls=%async_computation | async-start | bytes 2097152 | tf_op jit(solution)/shard_map/all_to_all | solution.py:150
  17.8 7.5 %slice_bitcast_fusion.5 = (bf16[32,2,128,128]{3,2,1,0:T(8,128)(2,1)S(1)}, bf16[32,2,128,128]{3,2,1,0:T(8,128)(2,1)}, bf16[32,2,128,128]{3,2,1,0:T(8,128)(2,1)}, ...) fusion(bf16[5,1,1,32,2,128,128]{6,5,4,3,2,1,0:T(8,128)(2,1)} %param.6), kind=kLoop, calls=%fused_computation.5 | loop fusion | bytes 20971520 | tf_op jit(solution)/shard_map/squeeze | solution.py:152
  25.2 0.7 copy.9
  26.0 1.0 reshape.66.cols_other_ref
  27.0 7.6 %slice_bitcast_fusion = (bf16[32,2,128,128]{3,2,1,0:T(8,128)(2,1)}, bf16[32,2,128,128]{3,2,1,0:T(8,128)(2,1)}, bf16[32,2,128,128]{3,2,1,0:T(8,128)(2,1)}, bf16[3...) fusion(bf16[5,1,1,32,2,128,128]{6,5,4,3,2,1,0:T(8,128)(2,1)} %collective-permute-done.3), kind=kLoop, calls=%fused_computation | loop fusion | bytes 20971520 | tf_op jit(solution)/shard_map/squeeze | solution.py:152
  34.6 0.7 all-to-all-done.panels_ref
  35.3 1.6 copy-done.6
  36.9 1.6 copy-done.8
  38.5 2.5 level_terms.5
  41.0 24.2 %all_to_all.50.terms_ref = bf16[16,2,128,256]{3,2,1,0:T(8,128)(2,1)S(1)} all-to-all(bf16[16,2,128,256]{3,2,1,0:T(8,128)(2,1)S(1)} %level_terms.5), channel_id=1, replica_groups=mesh['chip'=16,'core'=2,'row'=8] {'chip'}, dimensions={0} | all-to-all | bytes 4194304 | tf_op jit(solution)/shard_map/all_to_all | solution.py:154
  65.9 23.6 %all_to_all.51.panels_ref = bf16[8,2,128,256]{3,2,1,0:T(8,128)(2,1)S(1)} all-to-all(bf16[8,2,128,256]{3,2,1,0:T(8,128)(2,1)S(1)} %get-tuple-element.26), channel_id=1, replica_groups=mesh['chip'=16,'core'=2,'row'=8] {'row'}, dimensions={0} | all-to-all | bytes 2097152 | tf_op jit(solution)/shard_map/all_to_all | solution.py:150
  89.5 2.4 level_terms.6
  91.9 20.3 %all_to_all.52.terms_ref = bf16[16,2,128,256]{3,2,1,0:T(8,128)(2,1)S(1)} all-to-all(bf16[16,2,128,256]{3,2,1,0:T(8,128)(2,1)S(1)} %level_terms.6), channel_id=1, replica_groups=mesh['chip'=16,'core'=2,'row'=8] {'chip'}, dimensions={0} | all-to-all | bytes 4194304 | tf_op jit(solution)/shard_map/all_to_all | solution.py:154
  112.9 20.3 %all_to_all.53.panels_ref = bf16[8,2,128,256]{3,2,1,0:T(8,128)(2,1)S(1)} all-to-all(bf16[8,2,128,256]{3,2,1,0:T(8,128)(2,1)S(1)} %get-tuple-element.28), channel_id=1, replica_groups=mesh['chip'=16,'core'=2,'row'=8] {'row'}, dimensions={0} | all-to-all | bytes 2097152 | tf_op jit(solution)/shard_map/all_to_all | solution.py:150
  133.2 2.4 level_terms.7
  135.6 20.3 %all_to_all.54.terms_ref = bf16[16,2,128,256]{3,2,1,0:T(8,128)(2,1)S(1)} all-to-all(bf16[16,2,128,256]{3,2,1,0:T(8,128)(2,1)S(1)} %level_terms.7), channel_id=1, replica_groups=mesh['chip'=16,'core'=2,'row'=8] {'chip'}, dimensions={0} | all-to-all | bytes 4194304 | tf_op jit(solution)/shard_map/all_to_all | solution.py:154
  156.6 20.3 %all_to_all.55.panels_ref = bf16[8,2,128,256]{3,2,1,0:T(8,128)(2,1)S(1)} all-to-all(bf16[8,2,128,256]{3,2,1,0:T(8,128)(2,1)S(1)} %get-tuple-element.30), channel_id=1, replica_groups=mesh['chip'=16,'core'=2,'row'=8] {'row'}, dimensions={0} | all-to-all | bytes 2097152 | tf_op jit(solution)/shard_map/all_to_all | solution.py:150
  176.9 2.4 level_terms.8
  179.3 20.3 %all_to_all.56.terms_ref = bf16[16,2,128,256]{3,2,1,0:T(8,128)(2,1)S(1)} all-to-all(bf16[16,2,128,256]{3,2,1,0:T(8,128)(2,1)S(1)} %level_terms.8), channel_id=1, replica_groups=mesh['chip'=16,'core'=2,'row'=8] {'chip'}, dimensions={0} | all-to-all | bytes 4194304 | tf_op jit(solution)/shard_map/all_to_all | solution.py:154
  200.3 20.5 %all_to_all.57.panels_ref = bf16[8,2,128,256]{3,2,1,0:T(8,128)(2,1)S(1)} all-to-all(bf16[8,2,128,256]{3,2,1,0:T(8,128)(2,1)S(1)} %get-tuple-element.32), channel_id=1, replica_groups=mesh['chip'=16,'core'=2,'row'=8] {'row'}, dimensions={0} | all-to-all | bytes 2097152 | tf_op jit(solution)/shard_map/all_to_all | solution.py:150
  220.8 2.4 level_terms.9
  223.2 1.3 copy-done.9
  224.6 3.8 %all-to-all-start.9 = ((bf16[16,2,128,256]{3,2,1,0:T(8,128)(2,1)}), bf16[16,2,128,256]{3,2,1,0:T(8,128)(2,1)S(1)}, u32[]{:S(2)}, u32[]{:S(2)}) async-start(bf16[16,2,128,256]{3,2,1,0:T(8,128)(2,1)} %copy-done.9), calls=%async_computation.9 | async-start | bytes 4194304 | tf_op jit(solution)/shard_map/all_to_all | solution.py:154
  231.6 23.8 %collective-permute-start.4 = (bf16[5,128,256]{2,1,0:T(8,128)(2,1)}, bf16[5,128,256]{2,1,0:T(8,128)(2,1)S(1)}, u32[]{:S(2)}, u32[]{:S(2)}) collective-permute-start(bf16[5,128,256]{2,1,0:T(8,128)(2,1)} %get-tuple-element.58), channel_id=1, source_target_pairs={{0,8},{8,0},{1,9},{9,1},{2,10},{10,2},{3,11},{11,3},{4,12},{12,4},... | collective-permute-start | bytes 983048 | tf_op jit(solution)/shard_map/ppermute | solution.py:158
  256.0 17.8 %collective-permute-start.5 = (bf16[1,128,256]{2,1,0:T(8,128)(2,1)S(1)}, bf16[1,128,256]{2,1,0:T(8,128)(2,1)S(1)}, u32[]{:S(2)}, u32[]{:S(2)}) collective-permute-start(bf16[1,128,256]{2,1,0:T(8,128)(2,1)S(1)} %get-tuple-element.68), channel_id=1, source_target_pairs={{0,8},{8,0},{1,9},{9,1},{2,10},{10,2},{3,11},{11,3},{4,12},{12,4},... | collective-permute-start | bytes 196616 | tf_op jit(solution)/shard_map/ppermute | solution.py:158
  274.8 0.9 maximum_bitcast_fusion
  (61 shorter events, 9.1 us)
Async XLA Ops:
  1.2 5.2 %collective-permute-start = (bf16[6,128,256]{2,1,0:T(8,128)(2,1)S(1)}, bf16[6,128,256]{2,1,0:T(8,128)(2,1)S(1)}, u32[]{:S(2)}, u32[]{:S(2)}) collective-permute-start(bf16[6,128,256]{2,1,0:T(8,128)(2,1)S(1)} %get-tuple-element.50), channel_id=1, source_target_pairs={{0,8},{8,0},{1,9},{9,1},{2,10},{10,2},{3,11},{11,3},{4,12},{12,4},... | collective-permute-start | bytes 1179656 | tf_op jit(solution)/shard_map/ppermute | solution.py:129
  4.5 1.9 collective-permute-start.1
  4.6 1.7 collective-permute-start.2
  6.4 20.7 %collective-permute-start.3 = (bf16[5,1,1,32,2,128,128]{6,5,4,3,2,1,0:T(8,128)(2,1)}, bf16[5,1,1,32,2,128,128]{6,5,4,3,2,1,0:T(8,128)(2,1)}, u32[]{:S(2)}, u32[]{:S(2)}) collective-permute-start(bf16[5,1,1,32,2,128,128]{6,5,4,3,2,1,0:T(8,128)(2,1)} %param.6), channel_id=1, source_target_pairs={{0,8},{8,0},{1,9},{9,1},{2,10},{10,2},{3,11},{11,3},{4,12},{12,4},... | collective-permute-start | bytes 31457288 | tf_op jit(solution)/shard_map/ppermute | solution.py:135
  8.3 9.2 %copy-start.19 = (s32[5,1,1,32,2]{3,4,2,1,0:T(2,128)S(1)}, s32[5,1,1,32,2]{3,4,2,1,0:T(2,128)}, u32[]{:S(2)}) copy-start(s32[5,1,1,32,2]{3,4,2,1,0:T(2,128)} %param.7) | copy-start | bytes 3844
  10.4 0.6 copy-start.17
  11.0 24.3 %all-to-all-start = ((bf16[8,2,128,256]{3,2,1,0:T(8,128)(2,1)}), bf16[8,2,128,256]{3,2,1,0:T(8,128)(2,1)S(1)}, u32[]{:S(2)}, u32[]{:S(2)}) async-start(bf16[8,2,128,256]{3,2,1,0:T(8,128)(2,1)} %get-tuple-element.23), calls=%async_computation | async-start | bytes 2097152 | tf_op jit(solution)/shard_map/all_to_all | solution.py:150
  35.3 1.6 copy-start.6
  36.9 1.6 copy-start.8
  41.0 24.3 %copy-start.11 = (bf16[2,128,256]{2,1,0:T(8,128)(2,1)S(1)}, bf16[2,128,256]{2,1,0:T(8,128)(2,1)}, u32[]{:S(2)}) copy-start(bf16[2,128,256]{2,1,0:T(8,128)(2,1)} %get-tuple-element.45.rhs_ref) | copy-start | bytes 393220
  41.0 24.3 %copy-start.16 = (bf16[2,128,128]{2,1,0:T(8,128)(2,1)S(1)}, bf16[2,128,128]{2,1,0:T(8,128)(2,1)}, u32[]{:S(2)}) copy-start(bf16[2,128,128]{2,1,0:T(8,128)(2,1)} %get-tuple-element.53.inv_ref) | copy-start | bytes 196612
  65.3 24.3 %copy-start.5 = (bf16[32,2,128,128]{3,2,1,0:T(8,128)(2,1)S(1)}, bf16[32,2,128,128]{3,2,1,0:T(8,128)(2,1)}, u32[]{:S(2)}) copy-start(bf16[32,2,128,128]{3,2,1,0:T(8,128)(2,1)} %get-tuple-element.40.mine_ref) | copy-start | bytes 6291460
  65.3 24.3 %copy-start.7 = (bf16[32,2,128,128]{3,2,1,0:T(8,128)(2,1)S(1)}, bf16[32,2,128,128]{3,2,1,0:T(8,128)(2,1)}, u32[]{:S(2)}) copy-start(bf16[32,2,128,128]{3,2,1,0:T(8,128)(2,1)} %get-tuple-element.36.other_ref) | copy-start | bytes 6291460
  91.9 20.3 %copy-start.10 = (bf16[2,128,256]{2,1,0:T(8,128)(2,1)S(1)}, bf16[2,128,256]{2,1,0:T(8,128)(2,1)}, u32[]{:S(2)}) copy-start(bf16[2,128,256]{2,1,0:T(8,128)(2,1)} %get-tuple-element.46.rhs_ref) | copy-start | bytes 393220
  91.9 20.3 %copy-start.15 = (bf16[2,128,128]{2,1,0:T(8,128)(2,1)S(1)}, bf16[2,128,128]{2,1,0:T(8,128)(2,1)}, u32[]{:S(2)}) copy-start(bf16[2,128,128]{2,1,0:T(8,128)(2,1)} %get-tuple-element.54.inv_ref) | copy-start | bytes 196612
  112.3 21.0 %copy-start.3 = (bf16[32,2,128,128]{3,2,1,0:T(8,128)(2,1)S(1)}, bf16[32,2,128,128]{3,2,1,0:T(8,128)(2,1)}, u32[]{:S(2)}) copy-start(bf16[32,2,128,128]{3,2,1,0:T(8,128)(2,1)} %get-tuple-element.39.mine_ref) | copy-start | bytes 6291460
  112.3 21.0 %copy-start.4 = (bf16[32,2,128,128]{3,2,1,0:T(8,128)(2,1)S(1)}, bf16[32,2,128,128]{3,2,1,0:T(8,128)(2,1)}, u32[]{:S(2)}) copy-start(bf16[32,2,128,128]{3,2,1,0:T(8,128)(2,1)} %get-tuple-element.35.other_ref) | copy-start | bytes 6291460
  135.6 20.3 %copy-start.14 = (bf16[2,128,128]{2,1,0:T(8,128)(2,1)S(1)}, bf16[2,128,128]{2,1,0:T(8,128)(2,1)}, u32[]{:S(2)}) copy-start(bf16[2,128,128]{2,1,0:T(8,128)(2,1)} %get-tuple-element.55.inv_ref) | copy-start | bytes 196612
  156.0 20.9 %copy-start.1 = (bf16[32,2,128,128]{3,2,1,0:T(8,128)(2,1)S(1)}, bf16[32,2,128,128]{3,2,1,0:T(8,128)(2,1)}, u32[]{:S(2)}) copy-start(bf16[32,2,128,128]{3,2,1,0:T(8,128)(2,1)} %get-tuple-element.42.mine_ref) | copy-start | bytes 6291460
  156.0 21.0 %copy-start.2 = (bf16[32,2,128,128]{3,2,1,0:T(8,128)(2,1)S(1)}, bf16[32,2,128,128]{3,2,1,0:T(8,128)(2,1)}, u32[]{:S(2)}) copy-start(bf16[32,2,128,128]{3,2,1,0:T(8,128)(2,1)} %get-tuple-element.34.other_ref) | copy-start | bytes 6291460
  179.3 20.3 %copy-start.13 = (bf16[2,128,128]{2,1,0:T(8,128)(2,1)S(1)}, bf16[2,128,128]{2,1,0:T(8,128)(2,1)}, u32[]{:S(2)}) copy-start(bf16[2,128,128]{2,1,0:T(8,128)(2,1)} %get-tuple-element.56.inv_ref) | copy-start | bytes 196612
  199.7 21.1 %copy-start = (bf16[32,2,128,128]{3,2,1,0:T(8,128)(2,1)S(1)}, bf16[32,2,128,128]{3,2,1,0:T(8,128)(2,1)}, u32[]{:S(2)}) copy-start(bf16[32,2,128,128]{3,2,1,0:T(8,128)(2,1)} %get-tuple-element.33.other_ref) | copy-start | bytes 6291460
  223.2 1.4 copy-start.9
  224.6 3.9 %copy-start.18 = (bf16[2,128,256]{2,1,0:T(8,128)(2,1)S(1)}, bf16[2,128,256]{2,1,0:T(8,128)(2,1)}, u32[]{:S(2)}) copy-start(bf16[2,128,256]{2,1,0:T(8,128)(2,1)} %copy-done.17) | copy-start | bytes 393220
  224.6 30.9 %copy-start.12 = (bf16[2,128,128]{2,1,0:T(8,128)(2,1)S(1)}, bf16[2,128,128]{2,1,0:T(8,128)(2,1)}, u32[]{:S(2)}) copy-start(bf16[2,128,128]{2,1,0:T(8,128)(2,1)} %get-tuple-element.51.inv_ref) | copy-start | bytes 196612
  224.6 30.9 %all-to-all-start.9 = ((bf16[16,2,128,256]{3,2,1,0:T(8,128)(2,1)}), bf16[16,2,128,256]{3,2,1,0:T(8,128)(2,1)S(1)}, u32[]{:S(2)}, u32[]{:S(2)}) async-start(bf16[16,2,128,256]{3,2,1,0:T(8,128)(2,1)} %copy-done.9), calls=%async_computation.9 | async-start | bytes 4194304 | tf_op jit(solution)/shard_map/all_to_all | solution.py:154
  231.6 42.2 %collective-permute-start.4 = (bf16[5,128,256]{2,1,0:T(8,128)(2,1)}, bf16[5,128,256]{2,1,0:T(8,128)(2,1)S(1)}, u32[]{:S(2)}, u32[]{:S(2)}) collective-permute-start(bf16[5,128,256]{2,1,0:T(8,128)(2,1)} %get-tuple-element.58), channel_id=1, source_target_pairs={{0,8},{8,0},{1,9},{9,1},{2,10},{10,2},{3,11},{11,3},{4,12},{12,4},... | collective-permute-start | bytes 983048 | tf_op jit(solution)/shard_map/ppermute | solution.py:158
  256.0 18.7 %collective-permute-start.5 = (bf16[1,128,256]{2,1,0:T(8,128)(2,1)S(1)}, bf16[1,128,256]{2,1,0:T(8,128)(2,1)S(1)}, u32[]{:S(2)}, u32[]{:S(2)}) collective-permute-start(bf16[1,128,256]{2,1,0:T(8,128)(2,1)S(1)} %get-tuple-element.68), channel_id=1, source_target_pairs={{0,8},{8,0},{1,9},{9,1},{2,10},{10,2},{3,11},{11,3},{4,12},{12,4},... | collective-permute-start | bytes 196616 | tf_op jit(solution)/shard_map/ppermute | solution.py:158

commit v3 on v2

--- a/solution.py
+++ b/solution.py
@@ -9,7 +9,7 @@
 from jax.sharding import PartitionSpec as P
 
 CORES = 2
-CHIP_BLOCK = 4
+CHIP_BLOCK = 8
 STAGGER = 36
 VMEM_LIMIT = 16 * 1024 * 1024
 VMEM = pl.BlockSpec(memory_space=pltpu.VMEM)
@@ -26,56 +26,61 @@
     return (dot(low) + dot(middle) + dot(high)).astype(jnp.bfloat16)
 
 
-def store_solved(slot, inverse, remainder, copies_ref, solved_ref):
+def store_solved(level, slot, inverse, remainder, solved_ref, copies_ref):
     panel = times_inverse(inverse, remainder)
-    solved_ref[slot] = panel
-    for peer in range(copies_ref.shape[0]):
-        copies_ref[peer, slot] = panel
+    solved_ref[level] = panel
+    if copies_ref is not None:
+        for peer in range(copies_ref.shape[0]):
+            copies_ref[peer, slot] = panel
 
 
-def first_kernel(core_ref, rhs_ref, inv_ref, copies_ref, solved_ref):
+def first_kernel(core_ref, rhs_ref, inv_ref, mine_ref, other_ref, copies_ref):
     def once(_, carry):
-        for slot in range(CORES):
-            store_solved(
-                slot, inv_ref[slot], rhs_ref[slot].astype(jnp.float32), copies_ref, solved_ref
-            )
+        for slot, solved_ref in enumerate((mine_ref, other_ref)):
+            remainder = rhs_ref[slot].astype(jnp.float32)
+            store_solved(0, slot, inv_ref[slot], remainder, solved_ref, copies_ref)
         return carry
 
     lax.fori_loop(0, 1 + (1 - core_ref[0]) * STAGGER, once, 0)
 
 
-def next_kernel(terms_ref, rhs_ref, inv_ref, *out_refs):
+def next_kernel(level, terms_ref, *refs):
+    rhs_refs, inv_refs, solved_refs = refs[:2], refs[2:4], refs[6:8]
+    copies_ref = refs[8] if len(refs) > 8 else None
     for slot in range(CORES):
         total = terms_ref[0, slot].astype(jnp.float32)
         for chip in range(1, terms_ref.shape[0]):
             total += terms_ref[chip, slot].astype(jnp.float32)
-        remainder = rhs_ref[slot].astype(jnp.float32) - total
-        if len(out_refs) == 2:
-            store_solved(slot, inv_ref[slot], remainder, *out_refs)
-        else:
-            out_refs[0][slot] = times_inverse(inv_ref[slot], remainder)
+        remainder = rhs_refs[slot][level].astype(jnp.float32) - total
+        store_solved(level, slot, inv_refs[slot][level], remainder, solved_refs[slot], copies_ref)
 
 
-def solve(core, terms, rhs, inv, peers):
-    solved = jax.ShapeDtypeStruct(rhs.shape, jnp.bfloat16)
-    copies = jax.ShapeDtypeStruct((peers, *rhs.shape), jnp.bfloat16)
-    if terms is None:
-        return pl.pallas_call(
-            first_kernel,
-            out_shape=(copies, solved),
-            in_specs=[SMEM, VMEM, VMEM],
-            out_specs=(VMEM, VMEM),
-            compiler_params=PARAMS,
-            name="first_panels",
-        )(core, rhs, inv)
+def first_solve(core, rhs, inv, levels, peers):
+    solved = jax.ShapeDtypeStruct((levels, *rhs.shape[1:]), jnp.bfloat16)
     return pl.pallas_call(
-        next_kernel,
-        out_shape=(copies, solved) if peers else solved,
-        in_specs=[VMEM, VMEM, VMEM],
-        out_specs=(VMEM, VMEM) if peers else VMEM,
+        first_kernel,
+        out_shape=(solved, solved, jax.ShapeDtypeStruct((peers, *rhs.shape), jnp.bfloat16)),
+        in_specs=[SMEM, VMEM, VMEM],
+        out_specs=(VMEM, VMEM, VMEM),
+        compiler_params=PARAMS,
+        name="first_panels",
+    )(core, rhs, inv)
+
+
+def solve(level, received, rhs, inv, solved, peers):
+    outs = [jax.ShapeDtypeStruct(x.shape, x.dtype) for x in solved]
+    if peers:
+        outs.append(jax.ShapeDtypeStruct((peers, *received.shape[1:]), jnp.bfloat16))
+    result = pl.pallas_call(
+        functools.partial(next_kernel, level),
+        out_shape=tuple(outs),
+        in_specs=[VMEM] * 7,
+        out_specs=(VMEM,) * len(outs),
+        input_output_aliases={5: 0, 6: 1},
         compiler_params=PARAMS,
         name="solve_panels",
-    )(terms, rhs, inv)
+    )(received, *rhs, *inv, *solved)
+    return result[:2], result[2] if peers else None
 
 
 def terms_kernel(level, core_ref, cols_ref, cols_other_ref, panels_ref, mine_ref, other_ref, out_ref):
@@ -133,36 +138,31 @@
         (factor, rhs_other, inv_other, columns_other)
     )
     factor_other = swap(large)
-    rhs_pair = jnp.stack([rhs_here, rhs_other], axis=1)
-    inv_pair = jnp.stack([diag_inv[:, 0, 0], inv_other[:, 0, 0]], axis=1)
     cols, cols_other = columns.reshape(-1), columns_other.reshape(-1)
+    rhs_all = (rhs_here, rhs_other)
+    inv_all = (diag_inv[:, 0, 0], inv_other[:, 0, 0])
 
-    solved = []
-    received = None
-    for level in range(levels):
-        last = level + 1 == levels
-        result = solve(core, received, rhs_pair[level], inv_pair[level], 0 if last else peers)
-        if last:
-            solved.append(result)
-            break
-        copies, panel = result
-        solved.append(panel)
+    mine, other, copies = first_solve(
+        core, jnp.stack([x[0] for x in rhs_all]), jnp.stack([x[0] for x in inv_all]), levels, peers
+    )
+    solved = (mine, other)
+    first_factors = factor[0, 0, 0], factor_other[0, 0, 0]
+    for level in range(levels - 1):
         panels = lax.all_to_all(copies, "row", 0, 0, tiled=True)
-        partial = terms(
-            level, core, cols, cols_other, panels, factor[level, 0, 0], factor_other[level, 0, 0]
+        factors = (
+            (factor[level, 0, 0], factor_other[level, 0, 0]) if level else first_factors
         )
+        partial = terms(level, core, cols, cols_other, panels, *factors)
         received = lax.all_to_all(partial, "chip", 0, 0, tiled=True)
+        last = level + 2 == levels
+        solved, copies = solve(level + 1, received, rhs_all, inv_all, solved, 0 if last else peers)
 
-    def whole(panels):
-        mine = jnp.stack([p[0] for p in panels])
-        other = swap(jnp.stack([p[1] for p in panels]))
-        return jnp.where(
-            here == 0,
-            jnp.concatenate([mine, other], axis=-1),
-            jnp.concatenate([other, mine], axis=-1),
-        )
-
-    out = jnp.concatenate([whole(solved[:-1]), whole(solved[-1:])], axis=0)
+    mine, other = solved[0], swap(solved[1])
+    out = jnp.where(
+        here == 0,
+        jnp.concatenate([mine, other], axis=-1),
+        jnp.concatenate([other, mine], axis=-1),
+    )
     return out[:, None, None]
 
 

time: 276 us -> 268 us (0.971)
  starting transfers between devices: 56.1 us -> 35.9 us
  blocking collectives: 170 us -> 188 us
  local copies, waits for them, and re-layouts: 26.6 us -> 22.6 us
  Pallas kernels: 16.6 us -> 13.8 us
    all_to_all x4 -> x5, blocking collectives: 85.2 us -> 105 us  [on_device(): received = lax.all_to_all(partial, 'chip', 0, 0, tiled=True)]
    ppermute x2 -> x1, starting transfers between devices: 41.6 us -> 25.3 us  [on_device(): mine, other = (solved[0], swap(solved[1]))]
    all_to_all x1 -> x0, starting transfers between devices: 3.85 us -> none  [on_device(): received = lax.all_to_all(partial, 'chip', 0, 0, tiled=True)]
    unnamed x45 -> x27, local copies, waits for them, and re-layouts: 7.89 us -> 4.33 us
  transfers between devices with their start and end apart: 8 -> 6, of which waited for: 3 -> 3; matrix products, arithmetic and copies ran while one was open for 8% -> 6% of each run, Pallas kernels for 1% -> 0%
where the time goes in v3:
time: 268 us; the launch traced here: 267 us
  blocking collectives  188 us (70%)
  starting transfers between devices  35.9 us (13%)
  local copies, waits for them, and re-layouts  22.6 us (8%)
  Pallas kernels  13.8 us (5%)
  waiting for transfers between devices  4.88 us (2%)
    all_to_all x5, blocking collectives, on_device(): received = lax.all_to_all(partial, 'chip', 0, 0, tiled=True)  105 us
    all_to_all x4, blocking collectives, on_device(): panels = lax.all_to_all(copies, 'row', 0, 0, tiled=True)  83.4 us
    ppermute x1, starting transfers between devices, on_device(): mine, other = (solved[0], swap(solved[1]))  25.3 us
    pallas_call x5, Pallas kernels, terms(): pl.pallas_call(functools.partial(terms_kernel, level), out_shape=jax.Shap...  10.3 us
    squeeze x1, local copies, waits for them, and re-layouts, on_device(): factor[level, 0, 0]  7.58 us
    squeeze x1, local copies, waits for them, and re-layouts, on_device(): factor_other[level, 0, 0]  7.52 us
    all_to_all x1, starting transfers between devices, on_device(): panels = lax.all_to_all(copies, 'row', 0, 0, tiled=True)  6.45 us
  transfers between devices with their start and end apart: 6, of which 3 were waited for; matrix products, arithmetic and copies ran while one was open for 6% of the time, Pallas kernels for 0%

profile of v3, /device:TPU:1, one launch (start us, length us, event | category | flops | bytes accessed | tf_op | source)
XLA Modules:
  0.0 266.9 jit_solution(1132965663820692926)
XLA Ops:
  0.0 1.2 dynamic-slice_bitcast_fusion
  1.2 3.3 %collective-permute-start = (bf16[6,128,256]{2,1,0:T(8,128)(2,1)S(1)}, bf16[6,128,256]{2,1,0:T(8,128)(2,1)S(1)}, u32[]{:S(2)}, u32[]{:S(2)}) collective-permute-start(bf16[6,128,256]{2,1,0:T(8,128)(2,1)S(1)} %get-tuple-element.58), channel_id=1, source_target_pairs={{0,8},{8,0},{1,9},{9,1},{2,10},{10,2},{3,11},{11,3},{4,12},{12,4},... | collective-permute-start | bytes 1179656 | tf_op jit(solution)/shard_map/ppermute | solution.py:134
  5.0 1.3 collective-permute-done.2
  6.7 0.8 dynamic-slice_bitcast_fusion.2
  7.6 0.8 slice_bitcast_fusion.11
  8.8 1.0 copy-done.11
  9.8 6.4 %all-to-all-start = ((bf16[8,2,128,256]{3,2,1,0:T(8,128)(2,1)}), bf16[8,2,128,256]{3,2,1,0:T(8,128)(2,1)S(1)}, u32[]{:S(2)}, u32[]{:S(2)}) async-start(bf16[8,2,128,256]{3,2,1,0:T(8,128)(2,1)} %copy-done.11), calls=%async_computation | async-start | bytes 2097152 | tf_op jit(solution)/shard_map/all_to_all | solution.py:151
  16.5 7.6 %slice_bitcast_fusion.5 = (bf16[32,2,128,128]{3,2,1,0:T(8,128)(2,1)}, bf16[32,2,128,128]{3,2,1,0:T(8,128)(2,1)}, bf16[32,2,128,128]{3,2,1,0:T(8,128)(2,1)}, bf16...) fusion(bf16[5,1,1,32,2,128,128]{6,5,4,3,2,1,0:T(8,128)(2,1)} %param.6), kind=kLoop, calls=%fused_computation.5 | loop fusion | bytes 20971520 | tf_op jit(solution)/shard_map/squeeze | solution.py:153
  24.3 7.5 %slice_bitcast_fusion = (bf16[32,2,128,128]{3,2,1,0:T(8,128)(2,1)}, bf16[32,2,128,128]{3,2,1,0:T(8,128)(2,1)}, bf16[32,2,128,128]{3,2,1,0:T(8,128)(2,1)}, bf16[3...) fusion(bf16[5,1,1,32,2,128,128]{6,5,4,3,2,1,0:T(8,128)(2,1)} %collective-permute-done.3), kind=kLoop, calls=%fused_computation | loop fusion | bytes 20971520 | tf_op jit(solution)/shard_map/squeeze | solution.py:153
  31.9 2.2 all-to-all-done.panels_ref
  34.0 1.6 copy-done.8
  35.6 1.6 copy-done.9
  37.2 2.1 level_terms.5
  39.3 24.2 %all_to_all.50.terms_ref = bf16[16,2,128,256]{3,2,1,0:T(8,128)(2,1)S(1)} all-to-all(bf16[16,2,128,256]{3,2,1,0:T(8,128)(2,1)S(1)} %level_terms.5), channel_id=1, replica_groups=mesh['chip'=16,'core'=2,'row'=8] {'chip'}, dimensions={0} | all-to-all | bytes 4194304 | tf_op jit(solution)/shard_map/all_to_all | solution.py:156
  63.5 0.6 solve_panels.5
  64.2 22.2 %all_to_all.51.panels_ref = bf16[8,2,128,256]{3,2,1,0:T(8,128)(2,1)S(1)} all-to-all(bf16[8,2,128,256]{3,2,1,0:T(8,128)(2,1)S(1)} %get-tuple-element.33), channel_id=1, replica_groups=mesh['chip'=16,'core'=2,'row'=8] {'row'}, dimensions={0} | all-to-all | bytes 2097152 | tf_op jit(solution)/shard_map/all_to_all | solution.py:151
  86.4 2.1 level_terms.6
  88.4 20.2 %all_to_all.52.terms_ref = bf16[16,2,128,256]{3,2,1,0:T(8,128)(2,1)S(1)} all-to-all(bf16[16,2,128,256]{3,2,1,0:T(8,128)(2,1)S(1)} %level_terms.6), channel_id=1, replica_groups=mesh['chip'=16,'core'=2,'row'=8] {'chip'}, dimensions={0} | all-to-all | bytes 4194304 | tf_op jit(solution)/shard_map/all_to_all | solution.py:156
  108.6 0.6 solve_panels.6
  109.3 20.3 %all_to_all.53.panels_ref = bf16[8,2,128,256]{3,2,1,0:T(8,128)(2,1)S(1)} all-to-all(bf16[8,2,128,256]{3,2,1,0:T(8,128)(2,1)S(1)} %get-tuple-element.36), channel_id=1, replica_groups=mesh['chip'=16,'core'=2,'row'=8] {'row'}, dimensions={0} | all-to-all | bytes 2097152 | tf_op jit(solution)/shard_map/all_to_all | solution.py:151
  129.6 2.1 level_terms.7
  131.7 20.2 %all_to_all.54.terms_ref = bf16[16,2,128,256]{3,2,1,0:T(8,128)(2,1)S(1)} all-to-all(bf16[16,2,128,256]{3,2,1,0:T(8,128)(2,1)S(1)} %level_terms.7), channel_id=1, replica_groups=mesh['chip'=16,'core'=2,'row'=8] {'chip'}, dimensions={0} | all-to-all | bytes 4194304 | tf_op jit(solution)/shard_map/all_to_all | solution.py:156
  151.9 0.6 solve_panels.7
  152.5 20.3 %all_to_all.55.panels_ref = bf16[8,2,128,256]{3,2,1,0:T(8,128)(2,1)S(1)} all-to-all(bf16[8,2,128,256]{3,2,1,0:T(8,128)(2,1)S(1)} %get-tuple-element.39), channel_id=1, replica_groups=mesh['chip'=16,'core'=2,'row'=8] {'row'}, dimensions={0} | all-to-all | bytes 2097152 | tf_op jit(solution)/shard_map/all_to_all | solution.py:151
  172.8 2.1 level_terms.8
  174.9 20.2 %all_to_all.56.terms_ref = bf16[16,2,128,256]{3,2,1,0:T(8,128)(2,1)S(1)} all-to-all(bf16[16,2,128,256]{3,2,1,0:T(8,128)(2,1)S(1)} %level_terms.8), channel_id=1, replica_groups=mesh['chip'=16,'core'=2,'row'=8] {'chip'}, dimensions={0} | all-to-all | bytes 4194304 | tf_op jit(solution)/shard_map/all_to_all | solution.py:156
  195.7 20.6 %all_to_all.57.panels_ref = bf16[8,2,128,256]{3,2,1,0:T(8,128)(2,1)S(1)} all-to-all(bf16[8,2,128,256]{3,2,1,0:T(8,128)(2,1)S(1)} %get-tuple-element.42), channel_id=1, replica_groups=mesh['chip'=16,'core'=2,'row'=8] {'row'}, dimensions={0} | all-to-all | bytes 2097152 | tf_op jit(solution)/shard_map/all_to_all | solution.py:151
  216.4 2.1 level_terms.9
  218.4 20.2 %all_to_all.58.terms_ref = bf16[16,2,128,256]{3,2,1,0:T(8,128)(2,1)S(1)} all-to-all(bf16[16,2,128,256]{3,2,1,0:T(8,128)(2,1)S(1)} %level_terms.9), channel_id=1, replica_groups=mesh['chip'=16,'core'=2,'row'=8] {'chip'}, dimensions={0} | all-to-all | bytes 4194304 | tf_op jit(solution)/shard_map/all_to_all | solution.py:156
  239.2 25.3 %collective-permute-start.4 = (bf16[6,128,256]{2,1,0:T(8,128)(2,1)S(1)}, bf16[6,128,256]{2,1,0:T(8,128)(2,1)S(1)}, u32[]{:S(2)}, u32[]{:S(2)}) collective-permute-start(bf16[6,128,256]{2,1,0:T(8,128)(2,1)S(1)} %get-tuple-element.46), channel_id=1, source_target_pairs={{0,8},{8,0},{1,9},{9,1},{2,10},{10,2},{3,11},{11,3},{4,12},{12,4},... | collective-permute-start | bytes 1179656 | tf_op jit(solution)/shard_map/ppermute | solution.py:160
  264.5 1.3 collective-permute-done.4
  265.8 1.1 fusion
  (40 shorter events, 3.1 us)
Async XLA Ops:
  0.0 16.2 %copy-start.12 = (s32[5,1,1,32,2]{3,4,2,1,0:T(2,128)S(1)}, s32[5,1,1,32,2]{3,4,2,1,0:T(2,128)}, u32[]{:S(2)}) copy-start(s32[5,1,1,32,2]{3,4,2,1,0:T(2,128)} %param.7) | copy-start | bytes 3844
  1.2 5.2 %collective-permute-start = (bf16[6,128,256]{2,1,0:T(8,128)(2,1)S(1)}, bf16[6,128,256]{2,1,0:T(8,128)(2,1)S(1)}, u32[]{:S(2)}, u32[]{:S(2)}) collective-permute-start(bf16[6,128,256]{2,1,0:T(8,128)(2,1)S(1)} %get-tuple-element.58), channel_id=1, source_target_pairs={{0,8},{8,0},{1,9},{9,1},{2,10},{10,2},{3,11},{11,3},{4,12},{12,4},... | collective-permute-start | bytes 1179656 | tf_op jit(solution)/shard_map/ppermute | solution.py:134
  4.5 1.9 collective-permute-start.1
  4.6 1.7 collective-permute-start.2
  6.4 18.0 %collective-permute-start.3 = (bf16[5,1,1,32,2,128,128]{6,5,4,3,2,1,0:T(8,128)(2,1)}, bf16[5,1,1,32,2,128,128]{6,5,4,3,2,1,0:T(8,128)(2,1)}, u32[]{:S(2)}, u32[]{:S(2)}) collective-permute-start(bf16[5,1,1,32,2,128,128]{6,5,4,3,2,1,0:T(8,128)(2,1)} %param.6), channel_id=1, source_target_pairs={{0,8},{8,0},{1,9},{9,1},{2,10},{10,2},{3,11},{11,3},{4,12},{12,4},... | collective-permute-start | bytes 31457288 | tf_op jit(solution)/shard_map/ppermute | solution.py:140
  8.8 1.0 copy-start.11
  9.8 24.3 %all-to-all-start = ((bf16[8,2,128,256]{3,2,1,0:T(8,128)(2,1)}), bf16[8,2,128,256]{3,2,1,0:T(8,128)(2,1)S(1)}, u32[]{:S(2)}, u32[]{:S(2)}) async-start(bf16[8,2,128,256]{3,2,1,0:T(8,128)(2,1)} %copy-done.11), calls=%async_computation | async-start | bytes 2097152 | tf_op jit(solution)/shard_map/all_to_all | solution.py:151
  34.0 1.6 copy-start.8
  35.6 1.6 copy-start.9
  39.3 24.2 %copy-start.10 = (bf16[6,1,1,128,128]{4,3,2,1,0:T(8,128)(2,1)S(1)}, bf16[6,1,1,128,128]{4,3,2,1,0:T(8,128)(2,1)}, u32[]{:S(2)}) copy-start(bf16[6,1,1,128,128]{4,3,2,1,0:T(8,128)(2,1)} %param.5) | copy-start | bytes 589828
  63.5 22.8 %copy-start.6 = (bf16[32,2,128,128]{3,2,1,0:T(8,128)(2,1)S(1)}, bf16[32,2,128,128]{3,2,1,0:T(8,128)(2,1)}, u32[]{:S(2)}) copy-start(bf16[32,2,128,128]{3,2,1,0:T(8,128)(2,1)} %get-tuple-element.54.mine_ref) | copy-start | bytes 6291460
  63.5 22.8 %copy-start.7 = (bf16[32,2,128,128]{3,2,1,0:T(8,128)(2,1)S(1)}, bf16[32,2,128,128]{3,2,1,0:T(8,128)(2,1)}, u32[]{:S(2)}) copy-start(bf16[32,2,128,128]{3,2,1,0:T(8,128)(2,1)} %get-tuple-element.50.other_ref) | copy-start | bytes 6291460
  108.6 21.0 %copy-start.4 = (bf16[32,2,128,128]{3,2,1,0:T(8,128)(2,1)S(1)}, bf16[32,2,128,128]{3,2,1,0:T(8,128)(2,1)}, u32[]{:S(2)}) copy-start(bf16[32,2,128,128]{3,2,1,0:T(8,128)(2,1)} %get-tuple-element.53.mine_ref) | copy-start | bytes 6291460
  108.6 21.0 %copy-start.5 = (bf16[32,2,128,128]{3,2,1,0:T(8,128)(2,1)S(1)}, bf16[32,2,128,128]{3,2,1,0:T(8,128)(2,1)}, u32[]{:S(2)}) copy-start(bf16[32,2,128,128]{3,2,1,0:T(8,128)(2,1)} %get-tuple-element.49.other_ref) | copy-start | bytes 6291460
  151.9 21.0 %copy-start.2 = (bf16[32,2,128,128]{3,2,1,0:T(8,128)(2,1)S(1)}, bf16[32,2,128,128]{3,2,1,0:T(8,128)(2,1)}, u32[]{:S(2)}) copy-start(bf16[32,2,128,128]{3,2,1,0:T(8,128)(2,1)} %get-tuple-element.56.mine_ref) | copy-start | bytes 6291460
  151.9 21.0 %copy-start.3 = (bf16[32,2,128,128]{3,2,1,0:T(8,128)(2,1)S(1)}, bf16[32,2,128,128]{3,2,1,0:T(8,128)(2,1)}, u32[]{:S(2)}) copy-start(bf16[32,2,128,128]{3,2,1,0:T(8,128)(2,1)} %get-tuple-element.48.other_ref) | copy-start | bytes 6291460
  195.1 21.3 %copy-start = (bf16[32,2,128,128]{3,2,1,0:T(8,128)(2,1)S(1)}, bf16[32,2,128,128]{3,2,1,0:T(8,128)(2,1)}, u32[]{:S(2)}) copy-start(bf16[32,2,128,128]{3,2,1,0:T(8,128)(2,1)} %get-tuple-element.52.mine_ref) | copy-start | bytes 6291460
  195.1 21.3 %copy-start.1 = (bf16[32,2,128,128]{3,2,1,0:T(8,128)(2,1)S(1)}, bf16[32,2,128,128]{3,2,1,0:T(8,128)(2,1)}, u32[]{:S(2)}) copy-start(bf16[32,2,128,128]{3,2,1,0:T(8,128)(2,1)} %get-tuple-element.47.other_ref) | copy-start | bytes 6291460
  239.2 26.6 %collective-permute-start.4 = (bf16[6,128,256]{2,1,0:T(8,128)(2,1)S(1)}, bf16[6,128,256]{2,1,0:T(8,128)(2,1)S(1)}, u32[]{:S(2)}, u32[]{:S(2)}) collective-permute-start(bf16[6,128,256]{2,1,0:T(8,128)(2,1)S(1)} %get-tuple-element.46), channel_id=1, source_target_pairs={{0,8},{8,0},{1,9},{9,1},{2,10},{10,2},{3,11},{11,3},{4,12},{12,4},... | collective-permute-start | bytes 1179656 | tf_op jit(solution)/shard_map/ppermute | solution.py:160

commit v4 on v3

--- a/solution.py
+++ b/solution.py
@@ -9,7 +9,8 @@
 from jax.sharding import PartitionSpec as P
 
 CORES = 2
-CHIP_BLOCK = 8
+RING_PARTS = 2
+CHIP_BLOCK = 16
 STAGGER = 36
 VMEM_LIMIT = 16 * 1024 * 1024
 VMEM = pl.BlockSpec(memory_space=pltpu.VMEM)
@@ -34,11 +35,12 @@
             copies_ref[peer, slot] = panel
 
 
-def first_kernel(core_ref, rhs_ref, inv_ref, mine_ref, other_ref, copies_ref):
+def first_kernel(core_ref, given_ref, mine_ref, other_ref, copies_ref):
     def once(_, carry):
         for slot, solved_ref in enumerate((mine_ref, other_ref)):
-            remainder = rhs_ref[slot].astype(jnp.float32)
-            store_solved(0, slot, inv_ref[slot], remainder, solved_ref, copies_ref)
+            half = solved_ref.shape[-1]
+            remainder = given_ref[slot, :, :half].astype(jnp.float32)
+            store_solved(0, slot, given_ref[slot, :, half:], remainder, solved_ref, copies_ref)
         return carry
 
     lax.fori_loop(0, 1 + (1 - core_ref[0]) * STAGGER, once, 0)
@@ -55,16 +57,22 @@
         store_solved(level, slot, inv_refs[slot][level], remainder, solved_refs[slot], copies_ref)
 
 
-def first_solve(core, rhs, inv, levels, peers):
-    solved = jax.ShapeDtypeStruct((levels, *rhs.shape[1:]), jnp.bfloat16)
+def first_solve(core, given, levels, peers):
+    _, blk, width = given.shape
+    half = width - blk
+    solved = jax.ShapeDtypeStruct((levels, blk, half), jnp.bfloat16)
     return pl.pallas_call(
         first_kernel,
-        out_shape=(solved, solved, jax.ShapeDtypeStruct((peers, *rhs.shape), jnp.bfloat16)),
-        in_specs=[SMEM, VMEM, VMEM],
+        out_shape=(
+            solved,
+            solved,
+            jax.ShapeDtypeStruct((peers, CORES, blk, half), jnp.bfloat16),
+        ),
+        in_specs=[SMEM, VMEM],
         out_specs=(VMEM, VMEM, VMEM),
         compiler_params=PARAMS,
         name="first_panels",
-    )(core, rhs, inv)
+    )(core, given)
 
 
 def solve(level, received, rhs, inv, solved, peers):
@@ -138,17 +146,24 @@
         (factor, rhs_other, inv_other, columns_other)
     )
     factor_other = swap(large)
-    cols, cols_other = columns.reshape(-1), columns_other.reshape(-1)
+    ring = peers // RING_PARTS
+    order = [part * ring + i for i in range(ring) for part in range(RING_PARTS)]
+    cols, cols_other = (
+        (x % ring * RING_PARTS + x // ring).reshape(-1) for x in (columns, columns_other)
+    )
     rhs_all = (rhs_here, rhs_other)
     inv_all = (diag_inv[:, 0, 0], inv_other[:, 0, 0])
 
+    first = [(x[0], y[0]) for x, y in zip(rhs_all, inv_all)]
     mine, other, copies = first_solve(
-        core, jnp.stack([x[0] for x in rhs_all]), jnp.stack([x[0] for x in inv_all]), levels, peers
+        core, jnp.stack([jnp.concatenate(x, axis=1) for x in first]), levels, peers
     )
     solved = (mine, other)
     first_factors = factor[0, 0, 0], factor_other[0, 0, 0]
     for level in range(levels - 1):
-        panels = lax.all_to_all(copies, "row", 0, 0, tiled=True)
+        panels = lax.all_to_all(
+            copies, "row", 0, 0, axis_index_groups=[order], tiled=True
+        )
         factors = (
             (factor[level, 0, 0], factor_other[level, 0, 0]) if level else first_factors
         )

time: 268 us -> 262 us (0.978)
  blocking collectives: 188 us -> 185 us
    all_to_all x4, blocking collectives: 83.4 us -> 80.1 us  [on_device(): lax.all_to_all(copies, 'row', 0, 0, axis_index_groups=[order], tiled=True)]
  transfers between devices with their start and end apart: 6 -> 6, of which waited for: 3 -> 2; matrix products, arithmetic and copies ran while one was open for 6% -> 7% of each run, Pallas kernels for 0% -> 0%
where the time goes in v4:
time: 262 us; the launch traced here: 261 us
  blocking collectives  185 us (71%)
  starting transfers between devices  36.1 us (14%)
  local copies, waits for them, and re-layouts  22.6 us (9%)
  Pallas kernels  13.1 us (5%)
  waiting for transfers between devices  2.7 us (1%)
    all_to_all x5, blocking collectives, on_device(): received = lax.all_to_all(partial, 'chip', 0, 0, tiled=True)  105 us
    all_to_all x4, blocking collectives, on_device(): lax.all_to_all(copies, 'row', 0, 0, axis_index_groups=[order], tiled=True)  80.1 us
    ppermute x1, starting transfers between devices, on_device(): mine, other = (solved[0], swap(solved[1]))  25.4 us
    pallas_call x5, Pallas kernels, terms(): pl.pallas_call(functools.partial(terms_kernel, level), out_shape=jax.Shap...  9.69 us
    squeeze x1, local copies, waits for them, and re-layouts, on_device(): factor[level, 0, 0]  7.58 us
    squeeze x1, local copies, waits for them, and re-layouts, on_device(): factor_other[level, 0, 0]  7.52 us
    all_to_all x1, starting transfers between devices, on_device(): lax.all_to_all(copies, 'row', 0, 0, axis_index_groups=[order], tiled=True)  6.45 us
  transfers between devices with their start and end apart: 6, of which 2 were waited for; matrix products, arithmetic and copies ran while one was open for 7% of the time, Pallas kernels for 0%

profile of v4, /device:TPU:1, one launch (start us, length us, event | category | flops | bytes accessed | tf_op | source)
XLA Modules:
  0.0 261.1 jit_solution(7666449051296948120)
XLA Ops:
  0.0 1.2 dynamic-slice_bitcast_fusion
  1.2 3.3 %collective-permute-start = (bf16[6,128,256]{2,1,0:T(8,128)(2,1)S(1)}, bf16[6,128,256]{2,1,0:T(8,128)(2,1)S(1)}, u32[]{:S(2)}, u32[]{:S(2)}) collective-permute-start(bf16[6,128,256]{2,1,0:T(8,128)(2,1)S(1)} %get-tuple-element.58), channel_id=1, source_target_pairs={{0,8},{8,0},{1,9},{9,1},{2,10},{10,2},{3,11},{11,3},{4,12},{12,4},... | collective-permute-start | bytes 1179656 | tf_op jit(solution)/shard_map/ppermute | solution.py:142
  5.0 1.3 collective-permute-done.2
  6.7 0.8 dynamic-slice_bitcast_fusion.2
  7.6 0.8 slice_bitcast_fusion.12
  8.8 1.0 copy-done.11
  9.8 6.4 %all-to-all-start = ((bf16[8,2,128,256]{3,2,1,0:T(8,128)(2,1)}), bf16[8,2,128,256]{3,2,1,0:T(8,128)(2,1)S(1)}, u32[]{:S(2)}, u32[]{:S(2)}) async-start(bf16[8,2,128,256]{3,2,1,0:T(8,128)(2,1)} %copy-done.11), calls=%async_computation | async-start | bytes 2097152 | tf_op jit(solution)/shard_map/all_to_all | solution.py:164
  16.6 7.6 %slice_bitcast_fusion.5 = (bf16[32,2,128,128]{3,2,1,0:T(8,128)(2,1)}, bf16[32,2,128,128]{3,2,1,0:T(8,128)(2,1)}, bf16[32,2,128,128]{3,2,1,0:T(8,128)(2,1)}, bf16...) fusion(bf16[5,1,1,32,2,128,128]{6,5,4,3,2,1,0:T(8,128)(2,1)} %param.6), kind=kLoop, calls=%fused_computation.5 | loop fusion | bytes 20971520 | tf_op jit(solution)/shard_map/squeeze | solution.py:168
  24.4 7.5 %slice_bitcast_fusion = (bf16[32,2,128,128]{3,2,1,0:T(8,128)(2,1)}, bf16[32,2,128,128]{3,2,1,0:T(8,128)(2,1)}, bf16[32,2,128,128]{3,2,1,0:T(8,128)(2,1)}, bf16[3...) fusion(bf16[5,1,1,32,2,128,128]{6,5,4,3,2,1,0:T(8,128)(2,1)} %collective-permute-done.3), kind=kLoop, calls=%fused_computation | loop fusion | bytes 20971520 | tf_op jit(solution)/shard_map/squeeze | solution.py:168
  32.0 1.6 copy-done.8
  33.6 1.6 copy-done.9
  35.1 2.1 level_terms.5
  37.3 24.2 %all_to_all.50.terms_ref = bf16[16,2,128,256]{3,2,1,0:T(8,128)(2,1)S(1)} all-to-all(bf16[16,2,128,256]{3,2,1,0:T(8,128)(2,1)S(1)} %level_terms.5), channel_id=1, replica_groups=mesh['chip'=16,'core'=2,'row'=8] {'chip'}, dimensions={0} | all-to-all | bytes 4194304 | tf_op jit(solution)/shard_map/all_to_all | solution.py:171
  61.5 0.6 solve_panels.5
  62.2 21.8 %all_to_all.51.panels_ref = bf16[8,2,128,256]{3,2,1,0:T(8,128)(2,1)S(1)} all-to-all(bf16[8,2,128,256]{3,2,1,0:T(8,128)(2,1)S(1)} %get-tuple-element.33), channel_id=1, replica_groups={{0,4,1,5,2,6,3,7},{8,12,9,13,10,14,11,15},{16,20,17,21,18,22,19,23},{24..., dimensions={0} | all-to-all | bytes 2097152 | tf_op jit(solution)/shard_map/all_to_all | solution.py:164
  84.0 1.9 level_terms.6
  85.9 20.2 %all_to_all.52.terms_ref = bf16[16,2,128,256]{3,2,1,0:T(8,128)(2,1)S(1)} all-to-all(bf16[16,2,128,256]{3,2,1,0:T(8,128)(2,1)S(1)} %level_terms.6), channel_id=1, replica_groups=mesh['chip'=16,'core'=2,'row'=8] {'chip'}, dimensions={0} | all-to-all | bytes 4194304 | tf_op jit(solution)/shard_map/all_to_all | solution.py:171
  106.1 0.6 solve_panels.6
  106.7 19.2 %all_to_all.53.panels_ref = bf16[8,2,128,256]{3,2,1,0:T(8,128)(2,1)S(1)} all-to-all(bf16[8,2,128,256]{3,2,1,0:T(8,128)(2,1)S(1)} %get-tuple-element.36), channel_id=1, replica_groups={{0,4,1,5,2,6,3,7},{8,12,9,13,10,14,11,15},{16,20,17,21,18,22,19,23},{24..., dimensions={0} | all-to-all | bytes 2097152 | tf_op jit(solution)/shard_map/all_to_all | solution.py:164
  125.9 1.9 level_terms.7
  127.8 20.2 %all_to_all.54.terms_ref = bf16[16,2,128,256]{3,2,1,0:T(8,128)(2,1)S(1)} all-to-all(bf16[16,2,128,256]{3,2,1,0:T(8,128)(2,1)S(1)} %level_terms.7), channel_id=1, replica_groups=mesh['chip'=16,'core'=2,'row'=8] {'chip'}, dimensions={0} | all-to-all | bytes 4194304 | tf_op jit(solution)/shard_map/all_to_all | solution.py:171
  148.0 0.6 solve_panels.7
  148.7 19.3 %all_to_all.55.panels_ref = bf16[8,2,128,256]{3,2,1,0:T(8,128)(2,1)S(1)} all-to-all(bf16[8,2,128,256]{3,2,1,0:T(8,128)(2,1)S(1)} %get-tuple-element.39), channel_id=1, replica_groups={{0,4,1,5,2,6,3,7},{8,12,9,13,10,14,11,15},{16,20,17,21,18,22,19,23},{24..., dimensions={0} | all-to-all | bytes 2097152 | tf_op jit(solution)/shard_map/all_to_all | solution.py:164
  168.0 1.9 level_terms.8
  169.9 20.4 %all_to_all.56.terms_ref = bf16[16,2,128,256]{3,2,1,0:T(8,128)(2,1)S(1)} all-to-all(bf16[16,2,128,256]{3,2,1,0:T(8,128)(2,1)S(1)} %level_terms.8), channel_id=1, replica_groups=mesh['chip'=16,'core'=2,'row'=8] {'chip'}, dimensions={0} | all-to-all | bytes 4194304 | tf_op jit(solution)/shard_map/all_to_all | solution.py:171
  190.3 0.6 solve_panels.8
  190.9 19.7 %all_to_all.57.panels_ref = bf16[8,2,128,256]{3,2,1,0:T(8,128)(2,1)S(1)} all-to-all(bf16[8,2,128,256]{3,2,1,0:T(8,128)(2,1)S(1)} %get-tuple-element.42), channel_id=1, replica_groups={{0,4,1,5,2,6,3,7},{8,12,9,13,10,14,11,15},{16,20,17,21,18,22,19,23},{24..., dimensions={0} | all-to-all | bytes 2097152 | tf_op jit(solution)/shard_map/all_to_all | solution.py:164
  210.7 1.9 level_terms.9
  212.6 20.2 %all_to_all.58.terms_ref = bf16[16,2,128,256]{3,2,1,0:T(8,128)(2,1)S(1)} all-to-all(bf16[16,2,128,256]{3,2,1,0:T(8,128)(2,1)S(1)} %level_terms.9), channel_id=1, replica_groups=mesh['chip'=16,'core'=2,'row'=8] {'chip'}, dimensions={0} | all-to-all | bytes 4194304 | tf_op jit(solution)/shard_map/all_to_all | solution.py:171
  233.3 25.4 %collective-permute-start.4 = (bf16[6,128,256]{2,1,0:T(8,128)(2,1)S(1)}, bf16[6,128,256]{2,1,0:T(8,128)(2,1)S(1)}, u32[]{:S(2)}, u32[]{:S(2)}) collective-permute-start(bf16[6,128,256]{2,1,0:T(8,128)(2,1)S(1)} %get-tuple-element.46), channel_id=1, source_target_pairs={{0,8},{8,0},{1,9},{9,1},{2,10},{10,2},{3,11},{11,3},{4,12},{12,4},... | collective-permute-start | bytes 1179656 | tf_op jit(solution)/shard_map/ppermute | solution.py:175
  258.7 1.3 collective-permute-done.4
  260.1 1.1 fusion
  (43 shorter events, 2.5 us)
Async XLA Ops:
  1.2 15.1 %copy-start.12 = (s32[5,1,1,32,2]{3,4,2,1,0:T(2,128)S(1)}, s32[5,1,1,32,2]{3,4,2,1,0:T(2,128)}, u32[]{:S(2)}) copy-start(s32[5,1,1,32,2]{3,4,2,1,0:T(2,128)} %param.7) | copy-start | bytes 3844
  1.2 5.2 %collective-permute-start = (bf16[6,128,256]{2,1,0:T(8,128)(2,1)S(1)}, bf16[6,128,256]{2,1,0:T(8,128)(2,1)S(1)}, u32[]{:S(2)}, u32[]{:S(2)}) collective-permute-start(bf16[6,128,256]{2,1,0:T(8,128)(2,1)S(1)} %get-tuple-element.58), channel_id=1, source_target_pairs={{0,8},{8,0},{1,9},{9,1},{2,10},{10,2},{3,11},{11,3},{4,12},{12,4},... | collective-permute-start | bytes 1179656 | tf_op jit(solution)/shard_map/ppermute | solution.py:142
  4.5 1.9 collective-permute-start.1
  4.6 1.7 collective-permute-start.2
  6.4 18.1 %collective-permute-start.3 = (bf16[5,1,1,32,2,128,128]{6,5,4,3,2,1,0:T(8,128)(2,1)}, bf16[5,1,1,32,2,128,128]{6,5,4,3,2,1,0:T(8,128)(2,1)}, u32[]{:S(2)}, u32[]{:S(2)}) collective-permute-start(bf16[5,1,1,32,2,128,128]{6,5,4,3,2,1,0:T(8,128)(2,1)} %param.6), channel_id=1, source_target_pairs={{0,8},{8,0},{1,9},{9,1},{2,10},{10,2},{3,11},{11,3},{4,12},{12,4},... | collective-permute-start | bytes 31457288 | tf_op jit(solution)/shard_map/ppermute | solution.py:148
  8.8 1.0 copy-start.11
  9.8 22.1 %all-to-all-start = ((bf16[8,2,128,256]{3,2,1,0:T(8,128)(2,1)}), bf16[8,2,128,256]{3,2,1,0:T(8,128)(2,1)S(1)}, u32[]{:S(2)}, u32[]{:S(2)}) async-start(bf16[8,2,128,256]{3,2,1,0:T(8,128)(2,1)} %copy-done.11), calls=%async_computation | async-start | bytes 2097152 | tf_op jit(solution)/shard_map/all_to_all | solution.py:164
  32.0 1.6 copy-start.8
  33.6 1.6 copy-start.9
  37.3 24.3 %copy-start.10 = (bf16[6,1,1,128,128]{4,3,2,1,0:T(8,128)(2,1)S(1)}, bf16[6,1,1,128,128]{4,3,2,1,0:T(8,128)(2,1)}, u32[]{:S(2)}) copy-start(bf16[6,1,1,128,128]{4,3,2,1,0:T(8,128)(2,1)} %param.5) | copy-start | bytes 589828
  61.5 22.4 %copy-start.6 = (bf16[32,2,128,128]{3,2,1,0:T(8,128)(2,1)S(1)}, bf16[32,2,128,128]{3,2,1,0:T(8,128)(2,1)}, u32[]{:S(2)}) copy-start(bf16[32,2,128,128]{3,2,1,0:T(8,128)(2,1)} %get-tuple-element.54.mine_ref) | copy-start | bytes 6291460
  61.5 22.4 %copy-start.7 = (bf16[32,2,128,128]{3,2,1,0:T(8,128)(2,1)S(1)}, bf16[32,2,128,128]{3,2,1,0:T(8,128)(2,1)}, u32[]{:S(2)}) copy-start(bf16[32,2,128,128]{3,2,1,0:T(8,128)(2,1)} %get-tuple-element.50.other_ref) | copy-start | bytes 6291460
  106.0 19.9 %copy-start.4 = (bf16[32,2,128,128]{3,2,1,0:T(8,128)(2,1)S(1)}, bf16[32,2,128,128]{3,2,1,0:T(8,128)(2,1)}, u32[]{:S(2)}) copy-start(bf16[32,2,128,128]{3,2,1,0:T(8,128)(2,1)} %get-tuple-element.53.mine_ref) | copy-start | bytes 6291460
  106.1 19.9 %copy-start.5 = (bf16[32,2,128,128]{3,2,1,0:T(8,128)(2,1)S(1)}, bf16[32,2,128,128]{3,2,1,0:T(8,128)(2,1)}, u32[]{:S(2)}) copy-start(bf16[32,2,128,128]{3,2,1,0:T(8,128)(2,1)} %get-tuple-element.49.other_ref) | copy-start | bytes 6291460
  148.0 20.0 %copy-start.2 = (bf16[32,2,128,128]{3,2,1,0:T(8,128)(2,1)S(1)}, bf16[32,2,128,128]{3,2,1,0:T(8,128)(2,1)}, u32[]{:S(2)}) copy-start(bf16[32,2,128,128]{3,2,1,0:T(8,128)(2,1)} %get-tuple-element.56.mine_ref) | copy-start | bytes 6291460
  148.0 20.0 %copy-start.3 = (bf16[32,2,128,128]{3,2,1,0:T(8,128)(2,1)S(1)}, bf16[32,2,128,128]{3,2,1,0:T(8,128)(2,1)}, u32[]{:S(2)}) copy-start(bf16[32,2,128,128]{3,2,1,0:T(8,128)(2,1)} %get-tuple-element.48.other_ref) | copy-start | bytes 6291460
  190.3 20.4 %copy-start = (bf16[32,2,128,128]{3,2,1,0:T(8,128)(2,1)S(1)}, bf16[32,2,128,128]{3,2,1,0:T(8,128)(2,1)}, u32[]{:S(2)}) copy-start(bf16[32,2,128,128]{3,2,1,0:T(8,128)(2,1)} %get-tuple-element.52.mine_ref) | copy-start | bytes 6291460
  190.3 20.4 %copy-start.1 = (bf16[32,2,128,128]{3,2,1,0:T(8,128)(2,1)S(1)}, bf16[32,2,128,128]{3,2,1,0:T(8,128)(2,1)}, u32[]{:S(2)}) copy-start(bf16[32,2,128,128]{3,2,1,0:T(8,128)(2,1)} %get-tuple-element.47.other_ref) | copy-start | bytes 6291460
  233.3 26.8 %collective-permute-start.4 = (bf16[6,128,256]{2,1,0:T(8,128)(2,1)S(1)}, bf16[6,128,256]{2,1,0:T(8,128)(2,1)S(1)}, u32[]{:S(2)}, u32[]{:S(2)}) collective-permute-start(bf16[6,128,256]{2,1,0:T(8,128)(2,1)S(1)} %get-tuple-element.46), channel_id=1, source_target_pairs={{0,8},{8,0},{1,9},{9,1},{2,10},{10,2},{3,11},{11,3},{4,12},{12,4},... | collective-permute-start | bytes 1179656 | tf_op jit(solution)/shard_map/ppermute | solution.py:175

commit v5 on v4

--- a/solution.py
+++ b/solution.py
@@ -11,7 +11,7 @@
 CORES = 2
 RING_PARTS = 2
 CHIP_BLOCK = 16
-STAGGER = 36
+STAGGER = 32
 VMEM_LIMIT = 16 * 1024 * 1024
 VMEM = pl.BlockSpec(memory_space=pltpu.VMEM)
 SMEM = pl.BlockSpec(memory_space=pltpu.SMEM)

time: 262 us -> 261 us (level)
  no operation moved by 1% of the time
where the time goes in v5:
time: 261 us; the launch traced here: 260 us
  blocking collectives  185 us (71%)
  starting transfers between devices  34.9 us (13%)
  local copies, waits for them, and re-layouts  22.6 us (9%)
  Pallas kernels  13.1 us (5%)
  waiting for transfers between devices  2.7 us (1%)
    all_to_all x5, blocking collectives, on_device(): received = lax.all_to_all(partial, 'chip', 0, 0, tiled=True)  106 us
    all_to_all x4, blocking collectives, on_device(): lax.all_to_all(copies, 'row', 0, 0, axis_index_groups=[order], tiled=True)  79.4 us
    ppermute x1, starting transfers between devices, on_device(): mine, other = (solved[0], swap(solved[1]))  24.2 us
    pallas_call x5, Pallas kernels, terms(): pl.pallas_call(functools.partial(terms_kernel, level), out_shape=jax.Shap...  9.69 us
    squeeze x1, local copies, waits for them, and re-layouts, on_device(): factor[level, 0, 0]  7.58 us
    squeeze x1, local copies, waits for them, and re-layouts, on_device(): factor_other[level, 0, 0]  7.52 us
    all_to_all x1, starting transfers between devices, on_device(): lax.all_to_all(copies, 'row', 0, 0, axis_index_groups=[order], tiled=True)  6.45 us
  transfers between devices with their start and end apart: 6, of which 2 were waited for; matrix products, arithmetic and copies ran while one was open for 7% of the time, Pallas kernels for 0%

profile of v5, /device:TPU:1, one launch (start us, length us, event | category | flops | bytes accessed | tf_op | source)
XLA Modules:
  0.0 259.7 jit_solution(17994305626646277378)
XLA Ops:
  0.0 1.2 dynamic-slice_bitcast_fusion
  1.2 3.3 %collective-permute-start = (bf16[6,128,256]{2,1,0:T(8,128)(2,1)S(1)}, bf16[6,128,256]{2,1,0:T(8,128)(2,1)S(1)}, u32[]{:S(2)}, u32[]{:S(2)}) collective-permute-start(bf16[6,128,256]{2,1,0:T(8,128)(2,1)S(1)} %get-tuple-element.58), channel_id=1, source_target_pairs={{0,8},{8,0},{1,9},{9,1},{2,10},{10,2},{3,11},{11,3},{4,12},{12,4},... | collective-permute-start | bytes 1179656 | tf_op jit(solution)/shard_map/ppermute | solution.py:142
  5.0 1.3 collective-permute-done.2
  6.7 0.8 dynamic-slice_bitcast_fusion.2
  7.6 0.8 slice_bitcast_fusion.12
  8.8 1.0 copy-done.11
  9.8 6.4 %all-to-all-start = ((bf16[8,2,128,256]{3,2,1,0:T(8,128)(2,1)}), bf16[8,2,128,256]{3,2,1,0:T(8,128)(2,1)S(1)}, u32[]{:S(2)}, u32[]{:S(2)}) async-start(bf16[8,2,128,256]{3,2,1,0:T(8,128)(2,1)} %copy-done.11), calls=%async_computation | async-start | bytes 2097152 | tf_op jit(solution)/shard_map/all_to_all | solution.py:164
  16.6 7.6 %slice_bitcast_fusion.5 = (bf16[32,2,128,128]{3,2,1,0:T(8,128)(2,1)}, bf16[32,2,128,128]{3,2,1,0:T(8,128)(2,1)}, bf16[32,2,128,128]{3,2,1,0:T(8,128)(2,1)}, bf16...) fusion(bf16[5,1,1,32,2,128,128]{6,5,4,3,2,1,0:T(8,128)(2,1)} %param.6), kind=kLoop, calls=%fused_computation.5 | loop fusion | bytes 20971520 | tf_op jit(solution)/shard_map/squeeze | solution.py:168
  24.4 7.5 %slice_bitcast_fusion = (bf16[32,2,128,128]{3,2,1,0:T(8,128)(2,1)}, bf16[32,2,128,128]{3,2,1,0:T(8,128)(2,1)}, bf16[32,2,128,128]{3,2,1,0:T(8,128)(2,1)}, bf16[3...) fusion(bf16[5,1,1,32,2,128,128]{6,5,4,3,2,1,0:T(8,128)(2,1)} %collective-permute-done.3), kind=kLoop, calls=%fused_computation | loop fusion | bytes 20971520 | tf_op jit(solution)/shard_map/squeeze | solution.py:168
  32.0 1.6 copy-done.8
  33.6 1.6 copy-done.9
  35.1 2.1 level_terms.5
  37.3 24.6 %all_to_all.50.terms_ref = bf16[16,2,128,256]{3,2,1,0:T(8,128)(2,1)S(1)} all-to-all(bf16[16,2,128,256]{3,2,1,0:T(8,128)(2,1)S(1)} %level_terms.5), channel_id=1, replica_groups=mesh['chip'=16,'core'=2,'row'=8] {'chip'}, dimensions={0} | all-to-all | bytes 4194304 | tf_op jit(solution)/shard_map/all_to_all | solution.py:171
  61.9 0.6 solve_panels.5
  62.5 21.6 %all_to_all.51.panels_ref = bf16[8,2,128,256]{3,2,1,0:T(8,128)(2,1)S(1)} all-to-all(bf16[8,2,128,256]{3,2,1,0:T(8,128)(2,1)S(1)} %get-tuple-element.33), channel_id=1, replica_groups={{0,4,1,5,2,6,3,7},{8,12,9,13,10,14,11,15},{16,20,17,21,18,22,19,23},{24..., dimensions={0} | all-to-all | bytes 2097152 | tf_op jit(solution)/shard_map/all_to_all | solution.py:164
  84.1 1.9 level_terms.6
  86.0 20.2 %all_to_all.52.terms_ref = bf16[16,2,128,256]{3,2,1,0:T(8,128)(2,1)S(1)} all-to-all(bf16[16,2,128,256]{3,2,1,0:T(8,128)(2,1)S(1)} %level_terms.6), channel_id=1, replica_groups=mesh['chip'=16,'core'=2,'row'=8] {'chip'}, dimensions={0} | all-to-all | bytes 4194304 | tf_op jit(solution)/shard_map/all_to_all | solution.py:171
  106.1 0.6 solve_panels.6
  106.8 19.2 %all_to_all.53.panels_ref = bf16[8,2,128,256]{3,2,1,0:T(8,128)(2,1)S(1)} all-to-all(bf16[8,2,128,256]{3,2,1,0:T(8,128)(2,1)S(1)} %get-tuple-element.36), channel_id=1, replica_groups={{0,4,1,5,2,6,3,7},{8,12,9,13,10,14,11,15},{16,20,17,21,18,22,19,23},{24..., dimensions={0} | all-to-all | bytes 2097152 | tf_op jit(solution)/shard_map/all_to_all | solution.py:164
  126.0 1.9 level_terms.7
  127.9 20.2 %all_to_all.54.terms_ref = bf16[16,2,128,256]{3,2,1,0:T(8,128)(2,1)S(1)} all-to-all(bf16[16,2,128,256]{3,2,1,0:T(8,128)(2,1)S(1)} %level_terms.7), channel_id=1, replica_groups=mesh['chip'=16,'core'=2,'row'=8] {'chip'}, dimensions={0} | all-to-all | bytes 4194304 | tf_op jit(solution)/shard_map/all_to_all | solution.py:171
  148.1 0.6 solve_panels.7
  148.8 19.3 %all_to_all.55.panels_ref = bf16[8,2,128,256]{3,2,1,0:T(8,128)(2,1)S(1)} all-to-all(bf16[8,2,128,256]{3,2,1,0:T(8,128)(2,1)S(1)} %get-tuple-element.39), channel_id=1, replica_groups={{0,4,1,5,2,6,3,7},{8,12,9,13,10,14,11,15},{16,20,17,21,18,22,19,23},{24..., dimensions={0} | all-to-all | bytes 2097152 | tf_op jit(solution)/shard_map/all_to_all | solution.py:164
  168.0 1.9 level_terms.8
  169.9 20.4 %all_to_all.56.terms_ref = bf16[16,2,128,256]{3,2,1,0:T(8,128)(2,1)S(1)} all-to-all(bf16[16,2,128,256]{3,2,1,0:T(8,128)(2,1)S(1)} %level_terms.8), channel_id=1, replica_groups=mesh['chip'=16,'core'=2,'row'=8] {'chip'}, dimensions={0} | all-to-all | bytes 4194304 | tf_op jit(solution)/shard_map/all_to_all | solution.py:171
  190.3 0.6 solve_panels.8
  190.9 19.3 %all_to_all.57.panels_ref = bf16[8,2,128,256]{3,2,1,0:T(8,128)(2,1)S(1)} all-to-all(bf16[8,2,128,256]{3,2,1,0:T(8,128)(2,1)S(1)} %get-tuple-element.42), channel_id=1, replica_groups={{0,4,1,5,2,6,3,7},{8,12,9,13,10,14,11,15},{16,20,17,21,18,22,19,23},{24..., dimensions={0} | all-to-all | bytes 2097152 | tf_op jit(solution)/shard_map/all_to_all | solution.py:164
  210.2 1.9 level_terms.9
  212.1 20.3 %all_to_all.58.terms_ref = bf16[16,2,128,256]{3,2,1,0:T(8,128)(2,1)S(1)} all-to-all(bf16[16,2,128,256]{3,2,1,0:T(8,128)(2,1)S(1)} %level_terms.9), channel_id=1, replica_groups=mesh['chip'=16,'core'=2,'row'=8] {'chip'}, dimensions={0} | all-to-all | bytes 4194304 | tf_op jit(solution)/shard_map/all_to_all | solution.py:171
  233.0 24.2 %collective-permute-start.4 = (bf16[6,128,256]{2,1,0:T(8,128)(2,1)S(1)}, bf16[6,128,256]{2,1,0:T(8,128)(2,1)S(1)}, u32[]{:S(2)}, u32[]{:S(2)}) collective-permute-start(bf16[6,128,256]{2,1,0:T(8,128)(2,1)S(1)} %get-tuple-element.46), channel_id=1, source_target_pairs={{0,8},{8,0},{1,9},{9,1},{2,10},{10,2},{3,11},{11,3},{4,12},{12,4},... | collective-permute-start | bytes 1179656 | tf_op jit(solution)/shard_map/ppermute | solution.py:175
  257.2 1.3 collective-permute-done.4
  258.6 1.1 fusion
  (43 shorter events, 2.5 us)
Async XLA Ops:
  1.2 15.1 %copy-start.12 = (s32[5,1,1,32,2]{3,4,2,1,0:T(2,128)S(1)}, s32[5,1,1,32,2]{3,4,2,1,0:T(2,128)}, u32[]{:S(2)}) copy-start(s32[5,1,1,32,2]{3,4,2,1,0:T(2,128)} %param.7) | copy-start | bytes 3844
  1.2 5.2 %collective-permute-start = (bf16[6,128,256]{2,1,0:T(8,128)(2,1)S(1)}, bf16[6,128,256]{2,1,0:T(8,128)(2,1)S(1)}, u32[]{:S(2)}, u32[]{:S(2)}) collective-permute-start(bf16[6,128,256]{2,1,0:T(8,128)(2,1)S(1)} %get-tuple-element.58), channel_id=1, source_target_pairs={{0,8},{8,0},{1,9},{9,1},{2,10},{10,2},{3,11},{11,3},{4,12},{12,4},... | collective-permute-start | bytes 1179656 | tf_op jit(solution)/shard_map/ppermute | solution.py:142
  4.5 1.9 collective-permute-start.1
  4.6 1.7 collective-permute-start.2
  6.4 18.1 %collective-permute-start.3 = (bf16[5,1,1,32,2,128,128]{6,5,4,3,2,1,0:T(8,128)(2,1)}, bf16[5,1,1,32,2,128,128]{6,5,4,3,2,1,0:T(8,128)(2,1)}, u32[]{:S(2)}, u32[]{:S(2)}) collective-permute-start(bf16[5,1,1,32,2,128,128]{6,5,4,3,2,1,0:T(8,128)(2,1)} %param.6), channel_id=1, source_target_pairs={{0,8},{8,0},{1,9},{9,1},{2,10},{10,2},{3,11},{11,3},{4,12},{12,4},... | collective-permute-start | bytes 31457288 | tf_op jit(solution)/shard_map/ppermute | solution.py:148
  8.8 1.0 copy-start.11
  9.8 22.1 %all-to-all-start = ((bf16[8,2,128,256]{3,2,1,0:T(8,128)(2,1)}), bf16[8,2,128,256]{3,2,1,0:T(8,128)(2,1)S(1)}, u32[]{:S(2)}, u32[]{:S(2)}) async-start(bf16[8,2,128,256]{3,2,1,0:T(8,128)(2,1)} %copy-done.11), calls=%async_computation | async-start | bytes 2097152 | tf_op jit(solution)/shard_map/all_to_all | solution.py:164
  32.0 1.6 copy-start.8
  33.5 1.6 copy-start.9
  37.3 24.6 %copy-start.10 = (bf16[6,1,1,128,128]{4,3,2,1,0:T(8,128)(2,1)S(1)}, bf16[6,1,1,128,128]{4,3,2,1,0:T(8,128)(2,1)}, u32[]{:S(2)}) copy-start(bf16[6,1,1,128,128]{4,3,2,1,0:T(8,128)(2,1)} %param.5) | copy-start | bytes 589828
  61.9 22.2 %copy-start.6 = (bf16[32,2,128,128]{3,2,1,0:T(8,128)(2,1)S(1)}, bf16[32,2,128,128]{3,2,1,0:T(8,128)(2,1)}, u32[]{:S(2)}) copy-start(bf16[32,2,128,128]{3,2,1,0:T(8,128)(2,1)} %get-tuple-element.54.mine_ref) | copy-start | bytes 6291460
  61.9 22.2 %copy-start.7 = (bf16[32,2,128,128]{3,2,1,0:T(8,128)(2,1)S(1)}, bf16[32,2,128,128]{3,2,1,0:T(8,128)(2,1)}, u32[]{:S(2)}) copy-start(bf16[32,2,128,128]{3,2,1,0:T(8,128)(2,1)} %get-tuple-element.50.other_ref) | copy-start | bytes 6291460
  106.1 19.9 %copy-start.4 = (bf16[32,2,128,128]{3,2,1,0:T(8,128)(2,1)S(1)}, bf16[32,2,128,128]{3,2,1,0:T(8,128)(2,1)}, u32[]{:S(2)}) copy-start(bf16[32,2,128,128]{3,2,1,0:T(8,128)(2,1)} %get-tuple-element.53.mine_ref) | copy-start | bytes 6291460
  106.1 19.9 %copy-start.5 = (bf16[32,2,128,128]{3,2,1,0:T(8,128)(2,1)S(1)}, bf16[32,2,128,128]{3,2,1,0:T(8,128)(2,1)}, u32[]{:S(2)}) copy-start(bf16[32,2,128,128]{3,2,1,0:T(8,128)(2,1)} %get-tuple-element.49.other_ref) | copy-start | bytes 6291460
  148.1 19.9 %copy-start.2 = (bf16[32,2,128,128]{3,2,1,0:T(8,128)(2,1)S(1)}, bf16[32,2,128,128]{3,2,1,0:T(8,128)(2,1)}, u32[]{:S(2)}) copy-start(bf16[32,2,128,128]{3,2,1,0:T(8,128)(2,1)} %get-tuple-element.56.mine_ref) | copy-start | bytes 6291460
  148.1 19.9 %copy-start.3 = (bf16[32,2,128,128]{3,2,1,0:T(8,128)(2,1)S(1)}, bf16[32,2,128,128]{3,2,1,0:T(8,128)(2,1)}, u32[]{:S(2)}) copy-start(bf16[32,2,128,128]{3,2,1,0:T(8,128)(2,1)} %get-tuple-element.48.other_ref) | copy-start | bytes 6291460
  190.3 19.9 %copy-start = (bf16[32,2,128,128]{3,2,1,0:T(8,128)(2,1)S(1)}, bf16[32,2,128,128]{3,2,1,0:T(8,128)(2,1)}, u32[]{:S(2)}) copy-start(bf16[32,2,128,128]{3,2,1,0:T(8,128)(2,1)} %get-tuple-element.52.mine_ref) | copy-start | bytes 6291460
  190.3 19.9 %copy-start.1 = (bf16[32,2,128,128]{3,2,1,0:T(8,128)(2,1)S(1)}, bf16[32,2,128,128]{3,2,1,0:T(8,128)(2,1)}, u32[]{:S(2)}) copy-start(bf16[32,2,128,128]{3,2,1,0:T(8,128)(2,1)} %get-tuple-element.47.other_ref) | copy-start | bytes 6291460
  233.0 25.6 %collective-permute-start.4 = (bf16[6,128,256]{2,1,0:T(8,128)(2,1)S(1)}, bf16[6,128,256]{2,1,0:T(8,128)(2,1)S(1)}, u32[]{:S(2)}, u32[]{:S(2)}) collective-permute-start(bf16[6,128,256]{2,1,0:T(8,128)(2,1)S(1)} %get-tuple-element.46), channel_id=1, source_target_pairs={{0,8},{8,0},{1,9},{9,1},{2,10},{10,2},{3,11},{11,3},{4,12},{12,4},... | collective-permute-start | bytes 1179656 | tf_op jit(solution)/shard_map/ppermute | solution.py:175

commit v6 on v5

--- a/solution.py
+++ b/solution.py
@@ -11,7 +11,7 @@
 CORES = 2
 RING_PARTS = 2
 CHIP_BLOCK = 16
-STAGGER = 32
+STAGGER = 30
 VMEM_LIMIT = 16 * 1024 * 1024
 VMEM = pl.BlockSpec(memory_space=pltpu.VMEM)
 SMEM = pl.BlockSpec(memory_space=pltpu.SMEM)

time: 261 us -> 260 us (level)
  no operation moved by 1% of the time
where the time goes in v6:
time: 260 us; the launch traced here: 259 us
  blocking collectives  185 us (71%)
  starting transfers between devices  34.1 us (13%)
  local copies, waits for them, and re-layouts  22.6 us (9%)
  Pallas kernels  13.1 us (5%)
  waiting for transfers between devices  2.7 us (1%)
    all_to_all x5, blocking collectives, on_device(): received = lax.all_to_all(partial, 'chip', 0, 0, tiled=True)  105 us
    all_to_all x4, blocking collectives, on_device(): lax.all_to_all(copies, 'row', 0, 0, axis_index_groups=[order], tiled=True)  79.8 us
    ppermute x1, starting transfers between devices, on_device(): mine, other = (solved[0], swap(solved[1]))  23.4 us
    pallas_call x5, Pallas kernels, terms(): pl.pallas_call(functools.partial(terms_kernel, level), out_shape=jax.Shap...  9.69 us
    squeeze x1, local copies, waits for them, and re-layouts, on_device(): factor[level, 0, 0]  7.58 us
    squeeze x1, local copies, waits for them, and re-layouts, on_device(): factor_other[level, 0, 0]  7.52 us
    all_to_all x1, starting transfers between devices, on_device(): lax.all_to_all(copies, 'row', 0, 0, axis_index_groups=[order], tiled=True)  6.45 us
  transfers between devices with their start and end apart: 6, of which 2 were waited for; matrix products, arithmetic and copies ran while one was open for 7% of the time, Pallas kernels for 0%

profile of v6, /device:TPU:1, one launch (start us, length us, event | category | flops | bytes accessed | tf_op | source)
XLA Modules:
  0.0 259.0 jit_solution(4114150445480508785)
XLA Ops:
  0.0 1.2 dynamic-slice_bitcast_fusion
  1.2 3.3 %collective-permute-start = (bf16[6,128,256]{2,1,0:T(8,128)(2,1)S(1)}, bf16[6,128,256]{2,1,0:T(8,128)(2,1)S(1)}, u32[]{:S(2)}, u32[]{:S(2)}) collective-permute-start(bf16[6,128,256]{2,1,0:T(8,128)(2,1)S(1)} %get-tuple-element.58), channel_id=1, source_target_pairs={{0,8},{8,0},{1,9},{9,1},{2,10},{10,2},{3,11},{11,3},{4,12},{12,4},... | collective-permute-start | bytes 1179656 | tf_op jit(solution)/shard_map/ppermute | solution.py:142
  5.0 1.3 collective-permute-done.2
  6.7 0.8 dynamic-slice_bitcast_fusion.2
  7.6 0.8 slice_bitcast_fusion.12
  8.8 1.0 copy-done.11
  9.8 6.4 %all-to-all-start = ((bf16[8,2,128,256]{3,2,1,0:T(8,128)(2,1)}), bf16[8,2,128,256]{3,2,1,0:T(8,128)(2,1)S(1)}, u32[]{:S(2)}, u32[]{:S(2)}) async-start(bf16[8,2,128,256]{3,2,1,0:T(8,128)(2,1)} %copy-done.11), calls=%async_computation | async-start | bytes 2097152 | tf_op jit(solution)/shard_map/all_to_all | solution.py:164
  16.6 7.6 %slice_bitcast_fusion.5 = (bf16[32,2,128,128]{3,2,1,0:T(8,128)(2,1)}, bf16[32,2,128,128]{3,2,1,0:T(8,128)(2,1)}, bf16[32,2,128,128]{3,2,1,0:T(8,128)(2,1)}, bf16...) fusion(bf16[5,1,1,32,2,128,128]{6,5,4,3,2,1,0:T(8,128)(2,1)} %param.6), kind=kLoop, calls=%fused_computation.5 | loop fusion | bytes 20971520 | tf_op jit(solution)/shard_map/squeeze | solution.py:168
  24.4 7.5 %slice_bitcast_fusion = (bf16[32,2,128,128]{3,2,1,0:T(8,128)(2,1)}, bf16[32,2,128,128]{3,2,1,0:T(8,128)(2,1)}, bf16[32,2,128,128]{3,2,1,0:T(8,128)(2,1)}, bf16[3...) fusion(bf16[5,1,1,32,2,128,128]{6,5,4,3,2,1,0:T(8,128)(2,1)} %collective-permute-done.3), kind=kLoop, calls=%fused_computation | loop fusion | bytes 20971520 | tf_op jit(solution)/shard_map/squeeze | solution.py:168
  32.0 1.6 copy-done.8
  33.6 1.6 copy-done.9
  35.1 2.1 level_terms.5
  37.3 24.4 %all_to_all.50.terms_ref = bf16[16,2,128,256]{3,2,1,0:T(8,128)(2,1)S(1)} all-to-all(bf16[16,2,128,256]{3,2,1,0:T(8,128)(2,1)S(1)} %level_terms.5), channel_id=1, replica_groups=mesh['chip'=16,'core'=2,'row'=8] {'chip'}, dimensions={0} | all-to-all | bytes 4194304 | tf_op jit(solution)/shard_map/all_to_all | solution.py:171
  61.7 0.6 solve_panels.5
  62.3 21.7 %all_to_all.51.panels_ref = bf16[8,2,128,256]{3,2,1,0:T(8,128)(2,1)S(1)} all-to-all(bf16[8,2,128,256]{3,2,1,0:T(8,128)(2,1)S(1)} %get-tuple-element.33), channel_id=1, replica_groups={{0,4,1,5,2,6,3,7},{8,12,9,13,10,14,11,15},{16,20,17,21,18,22,19,23},{24..., dimensions={0} | all-to-all | bytes 2097152 | tf_op jit(solution)/shard_map/all_to_all | solution.py:164
  84.1 1.9 level_terms.6
  86.0 20.2 %all_to_all.52.terms_ref = bf16[16,2,128,256]{3,2,1,0:T(8,128)(2,1)S(1)} all-to-all(bf16[16,2,128,256]{3,2,1,0:T(8,128)(2,1)S(1)} %level_terms.6), channel_id=1, replica_groups=mesh['chip'=16,'core'=2,'row'=8] {'chip'}, dimensions={0} | all-to-all | bytes 4194304 | tf_op jit(solution)/shard_map/all_to_all | solution.py:171
  106.2 0.6 solve_panels.6
  106.8 19.2 %all_to_all.53.panels_ref = bf16[8,2,128,256]{3,2,1,0:T(8,128)(2,1)S(1)} all-to-all(bf16[8,2,128,256]{3,2,1,0:T(8,128)(2,1)S(1)} %get-tuple-element.36), channel_id=1, replica_groups={{0,4,1,5,2,6,3,7},{8,12,9,13,10,14,11,15},{16,20,17,21,18,22,19,23},{24..., dimensions={0} | all-to-all | bytes 2097152 | tf_op jit(solution)/shard_map/all_to_all | solution.py:164
  126.0 1.9 level_terms.7
  127.9 20.2 %all_to_all.54.terms_ref = bf16[16,2,128,256]{3,2,1,0:T(8,128)(2,1)S(1)} all-to-all(bf16[16,2,128,256]{3,2,1,0:T(8,128)(2,1)S(1)} %level_terms.7), channel_id=1, replica_groups=mesh['chip'=16,'core'=2,'row'=8] {'chip'}, dimensions={0} | all-to-all | bytes 4194304 | tf_op jit(solution)/shard_map/all_to_all | solution.py:171
  148.1 0.6 solve_panels.7
  148.8 19.3 %all_to_all.55.panels_ref = bf16[8,2,128,256]{3,2,1,0:T(8,128)(2,1)S(1)} all-to-all(bf16[8,2,128,256]{3,2,1,0:T(8,128)(2,1)S(1)} %get-tuple-element.39), channel_id=1, replica_groups={{0,4,1,5,2,6,3,7},{8,12,9,13,10,14,11,15},{16,20,17,21,18,22,19,23},{24..., dimensions={0} | all-to-all | bytes 2097152 | tf_op jit(solution)/shard_map/all_to_all | solution.py:164
  168.0 1.9 level_terms.8
  169.9 20.4 %all_to_all.56.terms_ref = bf16[16,2,128,256]{3,2,1,0:T(8,128)(2,1)S(1)} all-to-all(bf16[16,2,128,256]{3,2,1,0:T(8,128)(2,1)S(1)} %level_terms.8), channel_id=1, replica_groups=mesh['chip'=16,'core'=2,'row'=8] {'chip'}, dimensions={0} | all-to-all | bytes 4194304 | tf_op jit(solution)/shard_map/all_to_all | solution.py:171
  190.3 0.6 solve_panels.8
  190.9 19.5 %all_to_all.57.panels_ref = bf16[8,2,128,256]{3,2,1,0:T(8,128)(2,1)S(1)} all-to-all(bf16[8,2,128,256]{3,2,1,0:T(8,128)(2,1)S(1)} %get-tuple-element.42), channel_id=1, replica_groups={{0,4,1,5,2,6,3,7},{8,12,9,13,10,14,11,15},{16,20,17,21,18,22,19,23},{24..., dimensions={0} | all-to-all | bytes 2097152 | tf_op jit(solution)/shard_map/all_to_all | solution.py:164
  210.5 1.9 level_terms.9
  212.4 20.2 %all_to_all.58.terms_ref = bf16[16,2,128,256]{3,2,1,0:T(8,128)(2,1)S(1)} all-to-all(bf16[16,2,128,256]{3,2,1,0:T(8,128)(2,1)S(1)} %level_terms.9), channel_id=1, replica_groups=mesh['chip'=16,'core'=2,'row'=8] {'chip'}, dimensions={0} | all-to-all | bytes 4194304 | tf_op jit(solution)/shard_map/all_to_all | solution.py:171
  233.1 23.4 %collective-permute-start.4 = (bf16[6,128,256]{2,1,0:T(8,128)(2,1)S(1)}, bf16[6,128,256]{2,1,0:T(8,128)(2,1)S(1)}, u32[]{:S(2)}, u32[]{:S(2)}) collective-permute-start(bf16[6,128,256]{2,1,0:T(8,128)(2,1)S(1)} %get-tuple-element.46), channel_id=1, source_target_pairs={{0,8},{8,0},{1,9},{9,1},{2,10},{10,2},{3,11},{11,3},{4,12},{12,4},... | collective-permute-start | bytes 1179656 | tf_op jit(solution)/shard_map/ppermute | solution.py:175
  256.5 1.3 collective-permute-done.4
  257.9 1.1 fusion
  (43 shorter events, 2.5 us)
Async XLA Ops:
  1.2 15.1 %copy-start.12 = (s32[5,1,1,32,2]{3,4,2,1,0:T(2,128)S(1)}, s32[5,1,1,32,2]{3,4,2,1,0:T(2,128)}, u32[]{:S(2)}) copy-start(s32[5,1,1,32,2]{3,4,2,1,0:T(2,128)} %param.7) | copy-start | bytes 3844
  1.2 5.2 %collective-permute-start = (bf16[6,128,256]{2,1,0:T(8,128)(2,1)S(1)}, bf16[6,128,256]{2,1,0:T(8,128)(2,1)S(1)}, u32[]{:S(2)}, u32[]{:S(2)}) collective-permute-start(bf16[6,128,256]{2,1,0:T(8,128)(2,1)S(1)} %get-tuple-element.58), channel_id=1, source_target_pairs={{0,8},{8,0},{1,9},{9,1},{2,10},{10,2},{3,11},{11,3},{4,12},{12,4},... | collective-permute-start | bytes 1179656 | tf_op jit(solution)/shard_map/ppermute | solution.py:142
  4.5 1.9 collective-permute-start.1
  4.6 1.7 collective-permute-start.2
  6.4 18.1 %collective-permute-start.3 = (bf16[5,1,1,32,2,128,128]{6,5,4,3,2,1,0:T(8,128)(2,1)}, bf16[5,1,1,32,2,128,128]{6,5,4,3,2,1,0:T(8,128)(2,1)}, u32[]{:S(2)}, u32[]{:S(2)}) collective-permute-start(bf16[5,1,1,32,2,128,128]{6,5,4,3,2,1,0:T(8,128)(2,1)} %param.6), channel_id=1, source_target_pairs={{0,8},{8,0},{1,9},{9,1},{2,10},{10,2},{3,11},{11,3},{4,12},{12,4},... | collective-permute-start | bytes 31457288 | tf_op jit(solution)/shard_map/ppermute | solution.py:148
  8.8 1.0 copy-start.11
  9.8 22.1 %all-to-all-start = ((bf16[8,2,128,256]{3,2,1,0:T(8,128)(2,1)}), bf16[8,2,128,256]{3,2,1,0:T(8,128)(2,1)S(1)}, u32[]{:S(2)}, u32[]{:S(2)}) async-start(bf16[8,2,128,256]{3,2,1,0:T(8,128)(2,1)} %copy-done.11), calls=%async_computation | async-start | bytes 2097152 | tf_op jit(solution)/shard_map/all_to_all | solution.py:164
  32.0 1.6 copy-start.8
  33.6 1.6 copy-start.9
  37.3 24.4 %copy-start.10 = (bf16[6,1,1,128,128]{4,3,2,1,0:T(8,128)(2,1)S(1)}, bf16[6,1,1,128,128]{4,3,2,1,0:T(8,128)(2,1)}, u32[]{:S(2)}) copy-start(bf16[6,1,1,128,128]{4,3,2,1,0:T(8,128)(2,1)} %param.5) | copy-start | bytes 589828
  61.7 22.4 %copy-start.6 = (bf16[32,2,128,128]{3,2,1,0:T(8,128)(2,1)S(1)}, bf16[32,2,128,128]{3,2,1,0:T(8,128)(2,1)}, u32[]{:S(2)}) copy-start(bf16[32,2,128,128]{3,2,1,0:T(8,128)(2,1)} %get-tuple-element.54.mine_ref) | copy-start | bytes 6291460
  61.7 22.4 %copy-start.7 = (bf16[32,2,128,128]{3,2,1,0:T(8,128)(2,1)S(1)}, bf16[32,2,128,128]{3,2,1,0:T(8,128)(2,1)}, u32[]{:S(2)}) copy-start(bf16[32,2,128,128]{3,2,1,0:T(8,128)(2,1)} %get-tuple-element.50.other_ref) | copy-start | bytes 6291460
  106.1 19.9 %copy-start.4 = (bf16[32,2,128,128]{3,2,1,0:T(8,128)(2,1)S(1)}, bf16[32,2,128,128]{3,2,1,0:T(8,128)(2,1)}, u32[]{:S(2)}) copy-start(bf16[32,2,128,128]{3,2,1,0:T(8,128)(2,1)} %get-tuple-element.53.mine_ref) | copy-start | bytes 6291460
  106.2 19.9 %copy-start.5 = (bf16[32,2,128,128]{3,2,1,0:T(8,128)(2,1)S(1)}, bf16[32,2,128,128]{3,2,1,0:T(8,128)(2,1)}, u32[]{:S(2)}) copy-start(bf16[32,2,128,128]{3,2,1,0:T(8,128)(2,1)} %get-tuple-element.49.other_ref) | copy-start | bytes 6291460
  148.1 19.9 %copy-start.2 = (bf16[32,2,128,128]{3,2,1,0:T(8,128)(2,1)S(1)}, bf16[32,2,128,128]{3,2,1,0:T(8,128)(2,1)}, u32[]{:S(2)}) copy-start(bf16[32,2,128,128]{3,2,1,0:T(8,128)(2,1)} %get-tuple-element.56.mine_ref) | copy-start | bytes 6291460
  148.1 19.9 %copy-start.3 = (bf16[32,2,128,128]{3,2,1,0:T(8,128)(2,1)S(1)}, bf16[32,2,128,128]{3,2,1,0:T(8,128)(2,1)}, u32[]{:S(2)}) copy-start(bf16[32,2,128,128]{3,2,1,0:T(8,128)(2,1)} %get-tuple-element.48.other_ref) | copy-start | bytes 6291460
  190.3 20.2 %copy-start = (bf16[32,2,128,128]{3,2,1,0:T(8,128)(2,1)S(1)}, bf16[32,2,128,128]{3,2,1,0:T(8,128)(2,1)}, u32[]{:S(2)}) copy-start(bf16[32,2,128,128]{3,2,1,0:T(8,128)(2,1)} %get-tuple-element.52.mine_ref) | copy-start | bytes 6291460
  190.3 20.2 %copy-start.1 = (bf16[32,2,128,128]{3,2,1,0:T(8,128)(2,1)S(1)}, bf16[32,2,128,128]{3,2,1,0:T(8,128)(2,1)}, u32[]{:S(2)}) copy-start(bf16[32,2,128,128]{3,2,1,0:T(8,128)(2,1)} %get-tuple-element.47.other_ref) | copy-start | bytes 6291460
  233.1 24.8 %collective-permute-start.4 = (bf16[6,128,256]{2,1,0:T(8,128)(2,1)S(1)}, bf16[6,128,256]{2,1,0:T(8,128)(2,1)S(1)}, u32[]{:S(2)}, u32[]{:S(2)}) collective-permute-start(bf16[6,128,256]{2,1,0:T(8,128)(2,1)S(1)} %get-tuple-element.46), channel_id=1, source_target_pairs={{0,8},{8,0},{1,9},{9,1},{2,10},{10,2},{3,11},{11,3},{4,12},{12,4},... | collective-permute-start | bytes 1179656 | tf_op jit(solution)/shard_map/ppermute | solution.py:175
